TPU v7x, 256 devices: a whole 4x4x8 slice. The times are simulated.
256 devices in a mesh: tm: 4 (over z_hi), tile: 64 (over y, x, z_lo, core).
Axes of the slice: x: 4, y: 4, z: 8 (z_hi: 4, z_lo: 2; z = z_hi * 2 + z_lo), core: 2. Of those that a mesh axis runs over, the one named last changes fastest.
Arguments:
- frames: bfloat16 [1024, 49152], P('tm', 'tile'), may hold values from -16 to 16
- segments: int32 [1024], replicated, may hold values from 0 to 2, as said below
- offset: int32 [1], replicated, may hold values from 0 to 45056
Outputs:
- instant: float32 [4096, 49152], P('tm', 'tile')
- lagged: float32 [4096, 49152], P('tm', 'tile')
Inputs may be any that keep to these rules, and one draw needn't show every extreme that they name: `segments`: each trajectory is a run of frames, in order of its id.
All inputs are finite; a program needn't handle non-finite values.
Results may differ from a plain program's by a relative error of at most 0.0036.
Values may be sent and summed in bfloat16 or wider, within the bound.
No kernel may reach another device: no remote copies, remote signals or barrier semaphores. Data moves between devices by JAX's collectives and lax.ppermute only.
A program may use at most 64 MiB of HBM per device.

v0:
```python
import jax
import jax.numpy as jnp
from jax import lax
from jax.sharding import PartitionSpec as P

S = 4096
LAG = 256


def broadcast(value, axis, root):
    mine = lax.axis_index(axis) == root
    return lax.psum(jnp.where(mine, value, jnp.zeros_like(value)), axis)


def center(values):
    total = values.shape[0]
    mean = jnp.sum(values, axis=0, dtype=jnp.float32) / total
    return (values.astype(jnp.float32) - mean).astype(jnp.bfloat16)


def shards(frames, segments, offset):
    columns = frames.shape[1]
    tiles = lax.axis_size("tile")
    start = offset[0]
    all_columns = lax.all_gather(frames, "tm", axis=0, tiled=True)
    first = start // columns
    count = min(tiles, (S - 1) // columns + 2)
    pieces = []
    for step in range(count):
        owner = jnp.minimum(first + step, tiles - 1)
        pieces.append(broadcast(frames, "tile", owner))
    joined = jnp.concatenate(pieces, axis=1)
    local_slab = lax.dynamic_slice_in_dim(joined, start - first * columns, S, 1)
    raw_slab = lax.all_to_all(local_slab, "tm", split_axis=1, concat_axis=0, tiled=True)
    total = all_columns.shape[0]
    centered = center(all_columns)
    slab = center(raw_slab)
    dims = (((0,), (0,)), ((), ()))
    instant = lax.dot_general(slab, centered, dims, preferred_element_type=jnp.float32) / total
    span = total - LAG
    valid = (segments[:span] == segments[LAG:]).astype(jnp.bfloat16)[:, None]
    pairs = jnp.sum(valid.astype(jnp.float32))
    left = jnp.concatenate([slab[:span], slab[LAG:]], axis=0)
    right = jnp.concatenate([centered[LAG:] * valid, centered[:span] * valid], axis=0)
    lagged = lax.dot_general(left, right, dims, preferred_element_type=jnp.float32) * 0.5 / pairs
    return (instant, lagged)


def solution(mesh):
    in_specs = (P("tm", "tile"), P(), P())
    out_specs = (P("tm", "tile"), P("tm", "tile"))
    return jax.shard_map(shards, mesh=mesh, in_specs=in_specs, out_specs=out_specs, check_vma=False)
```

profile of v0, /device:TPU:1, one launch (start us, length us, event | category | flops | bytes accessed | tf_op | source)
XLA Modules:
  0.0 672.8 jit_solution(16584525549358723453)
XLA Ops:
  8.0 0.0 all-reduce.3.cloned.1.call-start
  8.0 1.2 copy.5
  9.9 1.6 broadcast_select_fusion
  11.5 0.0 all-reduce.3.cloned.1.call-update
  11.5 0.0 all-gather.2.cloned.1.call-start
  11.6 0.5 all-gather.2.cloned.1.call-update
  12.1 573.1 %all-reduce.3.cloned.1.call-done = (bf16[256,768]{0,1:T(8,128)(2,1)}, bf16[256,768]{0,1:T(8,128)(2,1)}, bf16[256,768]{0,1:T(8,128)(2,1)}, bf16[256,768]{0,1:T(8,...) async-done(((bf16[256,768]{0,1:T(8,128)(2,1)}, bf16[256,768]{0,1:T(8,128)(2,1)}, bf16[256,768]{0,1:T(8,128)(2,1)}, ...) | async-done | bytes 2752528 | tf_op jit(solution)/shard_map/psum | solution.py:12
  585.2 0.0 copy-start.5
  585.2 0.0 copy-start.4
  585.2 0.0 copy-start.3
  585.2 1.1 constant_dynamic-update-slice_fusion.6
  586.3 1.0 constant_dynamic-update-slice_fusion.5
  587.4 1.0 constant_dynamic-update-slice_fusion.4
  588.4 1.0 constant_dynamic-update-slice_fusion.3
  589.4 0.0 copy-done.5
  589.5 0.0 copy-done.4
  589.5 0.0 copy-done.3
  589.6 1.9 constant_dynamic-slice_fusion
  591.4 0.0 copy-start.6
  591.4 5.9 all-to-all-start
  597.3 0.0 copy-done.6
  597.3 0.6 convert_reduce_fusion.2
  597.9 0.0 all-gather.2.cloned.1.call-done
  597.9 1.7 convert_reduce_fusion.1
  599.6 1.7 fusion.1
  601.3 0.0 copy-start
  601.3 1.1 copy-done
  602.4 1.3 slice_multiply_fusion.1
  603.8 40.9 %all-to-all-done = bf16[256,4,1024]{0,2,1:T(8,128)(2,1)S(1)} async-done(((bf16[256,4,1024]{0,2,1:T(8,128)(2,1)}), bf16[256,4,1024]{0,2,1:T(8,128)(2,1)S(1)}, u32[]{:S(2)}, u32[]{:S(2)}) %all-to-all-start) | async-done | bytes 2097184 | tf_op jit(solution)/shard_map/all_to_all | solution.py:34
  644.7 2.3 convert_bitcast_fusion
  647.0 5.4 copy.12
  652.4 0.3 convert_reduce_fusion
  652.7 0.0 copy-start.1
  652.7 2.9 fusion
  655.6 0.0 copy-done.1
  655.6 3.5 convolution_multiply_fusion
  659.2 0.0 copy-start.2
  659.2 0.4 fusion.16
  659.6 0.8 copy-done.2
  660.4 4.9 multiply_divide_fusion
  (5 shorter events, 0.1 us)
Async XLA Ops:
  8.0 577.2 %all-reduce.3.cloned.1.call-start = ((), (), s32[]{:S(2)}) async-start(), calls=%async_computation.2 | async-start | bytes 5505024 | tf_op jit(solution)/shard_map/psum | solution.py:12
  11.5 586.4 %all-gather.2.cloned.1.call-start = ((), (), s32[]{:S(2)}) async-start(), calls=%async_computation.1 | async-start | bytes 1966080 | tf_op jit(solution)/shard_map/all_gather | solution.py:25
  585.2 4.2 copy-start.5
  585.2 4.3 copy-start.4
  585.2 4.3 copy-start.3
  591.4 5.9 copy-start.6
  591.4 53.2 %all-to-all-start = ((bf16[256,4,1024]{0,2,1:T(8,128)(2,1)}), bf16[256,4,1024]{0,2,1:T(8,128)(2,1)S(1)}, u32[]{:S(2)}, u32[]{:S(2)}) async-start(bf16[256,4,1024]{0,2,1:T(8,128)(2,1)} %bitcast.14), calls=%async_computation | async-start | bytes 4194304 | tf_op jit(solution)/shard_map/all_to_all | solution.py:34
  601.3 1.1 copy-start
  652.7 2.9 copy-start.1
  659.2 1.3 copy-start.2
Sparse Core Ops, SparseCore 0:
  12.6 572.5 all-reduce.2
Sparse Core Ops, SparseCore 1:
  13.9 47.7 all-gather.1
where the time goes:
time: 674 us; the launch traced here: 673 us
  waiting for transfers between devices  615 us (91%)
  between operations  16.3 us (2%)
  local copies, waits for them, and re-layouts  15.1 us (2%)
  other arithmetic  12.4 us (2%)
  matrix products  8.43 us (1%)
    psum x1, waiting for transfers between devices, broadcast(): return lax.psum(jnp.where(mine, value, jnp.zeros_like(value)), axis)  573 us
    all_to_all x1, waiting for transfers between devices, shards(): lax.all_to_all(local_slab, 'tm', split_axis=1, concat_axis=0, tiled=True)  40.9 us
  transfers between devices with their start and end apart: 3, of which 2 were waited for; matrix products, arithmetic and copies ran while one was open for 2% of the time, Pallas kernels for 0%

commit v1 on v0

v1 whole, which is shorter than its diff:
```python
import jax
import jax.numpy as jnp
from jax import lax
from jax.experimental import pallas as pl
from jax.experimental.pallas import tpu as pltpu
from jax.sharding import Mesh, PartitionSpec as P

S = 4096
LAG = 256
FRAMES = 1024
W = 768
ROWS = 1024
AXES = ("tm", "y", "x", "zl", "core")
TILE = ("y", "x", "zl", "core")
F32 = jnp.float32
BF16 = jnp.bfloat16


def shift(value, axis, size, step):
    return lax.ppermute(value, axis, [(i, (i + step) % size) for i in range(size)])


def swap(value, axis):
    return lax.ppermute(value, axis, [(0, 1), (1, 0)])


def columns_kernel(place, own, next_lo, next_hi, prev_lo, prev_hi, far_lo, far_hi, valid, c_out, r_out, c_all):
    total = jnp.sum(own[...].astype(F32), axis=0, keepdims=True)
    for ref in (next_lo, next_hi, prev_lo, prev_hi, far_lo, far_hi):
        total += jnp.sum(ref[...].astype(F32), axis=0, keepdims=True)
    mean = total * (1.0 / FRAMES)
    c_all[0] = (own[...].astype(F32) - mean).astype(BF16)
    for d, lo, hi in ((1, next_lo, next_hi), (2, far_lo, far_hi), (3, prev_lo, prev_hi)):
        c_all[d, :128] = (lo[...].astype(F32) - mean).astype(BF16)
        c_all[d, 128:] = (hi[...].astype(F32) - mean).astype(BF16)
    for dc in range(2):
        for dy in range(4):
            core = lax.rem(place[1] + dc, 2)
            y = lax.rem(place[0] + dy, 4)
            rows = pl.ds(pl.multiple_of(core * 128 + y * 32, 32), 32)
            for d in range(4):
                c_out[dc, dy, d] = c_all[d, rows, :]
                after = c_all[(d + 1) % 4, rows, :].astype(F32) * valid[d, rows, :]
                before = c_all[(d + 3) % 4, rows, :].astype(F32) * valid[(d + 3) % 4, rows, :]
                r_out[dc, dy, d] = (after + before).astype(BF16)


def product_kernel(scale, *refs):
    slabs, c, r, instant, lagged, held = refs[:8], refs[8], refs[9], refs[10], refs[11], refs[12]
    total = jnp.zeros((1, held.shape[-1]), F32)
    for ref in slabs:
        total += jnp.sum(ref[...].astype(F32).reshape(128, -1), axis=0, keepdims=True)
    mean = total * (1.0 / FRAMES)
    for n, ref in enumerate(slabs):
        held[128 * n : 128 * n + 128] = (ref[...].reshape(128, -1).astype(F32) - mean).astype(BF16)
    dims = (((0,), (0,)), ((), ()))
    left = held[...]
    instant[...] = lax.dot_general(left, c[...], dims, preferred_element_type=F32) * (1.0 / FRAMES)
    lagged[...] = lax.dot_general(left, r[...], dims, preferred_element_type=F32) * scale[0]


def shards(frames, segments, offset):
    tm, y, x = lax.axis_index("tm"), lax.axis_index("y"), lax.axis_index("x")
    zl, core = lax.axis_index("zl"), lax.axis_index("core")
    start = offset[0]

    order = ("core", "y", "x", "zl")
    spread = lax.all_to_all(frames.reshape(64, 4, W), order, 0, 0, tiled=True).reshape(2, 32, 4, W)
    pair = jnp.minimum(start // (2 * W), 28)
    mine = lax.dynamic_slice(spread, (0, pair, 0, 0), (2, 4, 4, W))
    mine = mine.transpose(2, 1, 0, 3).reshape(4, 8 * W)
    mine = lax.dynamic_slice(mine, (0, start - pair * 2 * W), (4, S))

    lo, hi = frames[:128], frames[128:]
    prev_hi = shift(hi, "tm", 4, 1)
    next_lo = shift(lo, "tm", 4, -1)
    prev_lo = shift(lo, "tm", 4, 1)
    next_hi = shift(hi, "tm", 4, -1)
    far_hi = shift(prev_hi, "tm", 4, 1)
    far_lo = shift(next_lo, "tm", 4, -1)

    def block(d):
        return lax.dynamic_slice(mine, (0, lax.rem(tm + d, 4) * ROWS), (4, ROWS))

    got = [block(0)] + [shift(block(4 - d), "tm", 4, 4 - d) for d in (1, 2, 3)]
    part = jnp.stack(got)
    other = swap(part, "zl")
    first = zl == 0
    part = jnp.concatenate([jnp.where(first, part, other), jnp.where(first, other, part)], axis=1)
    rel = [part] + [shift(part, "x", 4, 4 - d) for d in (1, 2, 3)]
    nat = []
    for i in range(4):
        d = lax.rem(i - x + 4, 4)
        nat.append(jnp.where(d == 0, rel[0], jnp.where(d == 1, rel[1], jnp.where(d == 2, rel[2], rel[3]))))
    part = jnp.concatenate(nat, axis=1)
    own = [part] + [shift(part, "y", 4, 4 - d) for d in (1, 2, 3)]
    slabs = own + [swap(p, "core") for p in own]

    blocks = segments.reshape(4, LAG)
    valid = jnp.concatenate([blocks[:3] == blocks[1:], jnp.zeros((1, LAG), jnp.bool_)]).astype(F32)
    scale = (0.5 / jnp.sum(valid)).reshape(1)
    valid = lax.dynamic_slice(jnp.concatenate([valid, valid]), (tm, 0), (4, LAG))[:, :, None]

    vmem = pl.BlockSpec(memory_space=pltpu.VMEM)
    smem = pl.BlockSpec(memory_space=pltpu.SMEM)
    c, r = pl.pallas_call(
        columns_kernel,
        out_shape=[jax.ShapeDtypeStruct((2, 4, 4, 32, W), BF16)] * 2,
        in_specs=[smem] + [vmem] * 8,
        out_specs=[vmem] * 2,
        scratch_shapes=[pltpu.VMEM((4, LAG, W), BF16)],
        compiler_params=pltpu.CompilerParams(vmem_limit_bytes=24 * 2**20),
        cost_estimate=pl.CostEstimate(flops=10**7, bytes_accessed=6 * 2**20, transcendentals=0),
        name="columns",
    )(jnp.stack([y, core]), frames, next_lo, next_hi, prev_lo, prev_hi, far_lo, far_hi, valid)
    c, r = c.reshape(FRAMES, W), r.reshape(FRAMES, W)

    tile = 256
    outs = pl.pallas_call(
        product_kernel,
        grid=(ROWS // tile,),
        out_shape=[jax.ShapeDtypeStruct((ROWS, W), F32)] * 2,
        in_specs=[smem]
        + [pl.BlockSpec((4, 32, tile), lambda i: (0, 0, i))] * 8
        + [pl.BlockSpec((FRAMES, W), lambda i: (0, 0))] * 2,
        out_specs=[pl.BlockSpec((tile, W), lambda i: (i, 0))] * 2,
        scratch_shapes=[pltpu.VMEM((FRAMES, tile), BF16)],
        compiler_params=pltpu.CompilerParams(vmem_limit_bytes=32 * 2**20),
        cost_estimate=pl.CostEstimate(flops=4 * FRAMES * ROWS * W, bytes_accessed=12 * 2**20, transcendentals=0),
        name="products",
    )(scale, *slabs, c, r)
    return tuple(outs)


def solution(mesh):
    fine = Mesh(mesh.devices.reshape(4, 4, 4, 2, 2), AXES)
    cut = P("tm", TILE)
    return jax.shard_map(shards, mesh=fine, in_specs=(cut, P(), P()), out_specs=(cut, cut), check_vma=False)
```

time: 674 us -> 89.8 us (0.13)
  waiting for transfers between devices: 615 us -> 26.8 us
  starting transfers between devices: 5.98 us -> 48.7 us
  between operations: 16.3 us -> 2.2 us
  local copies, waits for them, and re-layouts: 15.1 us -> 2.44 us
  other arithmetic: 12.4 us -> 1.01 us
  matrix products: 8.43 us -> 0 us
  Pallas kernels: 0 us -> 8.37 us
    psum x1 -> x0, waiting for transfers between devices: 573 us -> none  [broadcast(): return lax.psum(jnp.where(mine, value, jnp.zeros_like(value)), axis)]
    ppermute x0 -> x20, starting transfers between devices: none -> 38.3 us  [the longest x15 27.8 us: shift(): lax.ppermute(value, axis, [(i, (i + step) % size) for i in range(size)])]
    all_to_all x1, waiting for transfers between devices: 40.9 us -> 9.93 us  [shards(): lax.all_to_all(frames.reshape(64, 4, W), order, 0, 0, tiled=True)]
    ppermute x0 -> x20, waiting for transfers between devices: none -> 16.8 us  [the longest x15 14.8 us: shift(): lax.ppermute(value, axis, [(i, (i + step) % size) for i in range(size)])]
    dot_general x2 -> x0, matrix products: 8.43 us -> none  [the longest x1 4.9 us: shards(): lax.dot_general(left, right, dims, preferred_element_type=jnp.float32) * 0.5]
    pallas_call x0 -> x2, Pallas kernels: none -> 8.37 us  [the longest x1 6.53 us: shards(): pl.pallas_call(product_kernel, grid=(ROWS // tile,), out_shape=[jax.Shape...]
    unnamed x21 -> x4, local copies, waits for them, and re-layouts: 7.38 us -> 0.01 us
    convert_element_type x3 -> x1, other arithmetic: 6.9 us -> 0.01 us  [shards(): jnp.concatenate([blocks[:3] == blocks[1:], jnp.zeros((1, LAG), jnp.bool_)])]
  transfers between devices with their start and end apart: 3 -> 21, of which waited for: 2 -> 8; matrix products, arithmetic and copies ran while one was open for 2% -> 1% of each run, Pallas kernels for 0% -> 2%
where the time goes in v1:
time: 89.8 us; the launch traced here: 89.5 us
  starting transfers between devices  48.7 us (54%)
  waiting for transfers between devices  26.8 us (30%)
  Pallas kernels  8.37 us (9%)
  local copies, waits for them, and re-layouts  2.44 us (3%)
  between operations  2.2 us (2%)
  other arithmetic  1.01 us (1%)
    ppermute x15, starting transfers between devices, shift(): lax.ppermute(value, axis, [(i, (i + step) % size) for i in range(size)])  27.8 us
    ppermute x15, waiting for transfers between devices, shift(): lax.ppermute(value, axis, [(i, (i + step) % size) for i in range(size)])  14.8 us
    ppermute x5, starting transfers between devices, swap(): return lax.ppermute(value, axis, [(0, 1), (1, 0)])  10.5 us
    all_to_all x1, starting transfers between devices, shards(): lax.all_to_all(frames.reshape(64, 4, W), order, 0, 0, tiled=True)  10.4 us
    all_to_all x1, waiting for transfers between devices, shards(): lax.all_to_all(frames.reshape(64, 4, W), order, 0, 0, tiled=True)  9.93 us
    pallas_call x1, Pallas kernels, shards(): pl.pallas_call(product_kernel, grid=(ROWS // tile,), out_shape=[jax.Shape...  6.53 us
    ppermute x5, waiting for transfers between devices, swap(): return lax.ppermute(value, axis, [(0, 1), (1, 0)])  2.02 us
    reshape x1, local copies, waits for them, and re-layouts, shards(): frames.reshape(64, 4, W)  1.89 us
  transfers between devices with their start and end apart: 21, of which 8 were waited for; matrix products, arithmetic and copies ran while one was open for 1% of the time, Pallas kernels for 2%

profile of v1, /device:TPU:1, one launch (start us, length us, event | category | flops | bytes accessed | tf_op | source)
XLA Modules:
  0.0 89.5 jit_solution(6712264400608418975)
XLA Ops:
  0.6 1.9 %reshape.43 = bf16[64,4,768]{2,1,0:T(4,128)(2,1)} reshape(bf16[256,768]{1,0:T(8,128)(2,1)} %own.1) | data formatting | bytes 786432 | tf_op jit(solution)/shard_map/reshape | solution.py:68
  2.5 10.4 %all-to-all-start = ((bf16[64,4,768]{2,1,0:T(4,128)(2,1)}), bf16[64,4,768]{2,1,0:T(4,128)(2,1)S(1)}, u32[]{:S(2)}, u32[]{:S(2)}) async-start(bf16[64,4,768]{2,1,0:T(4,128)(2,1)} %reshape.43), calls=%async_computation | async-start | bytes 786432 | tf_op jit(solution)/shard_map/all_to_all | solution.py:68
  13.7 9.9 %all-to-all-done = bf16[64,4,768]{2,1,0:T(4,128)(2,1)S(1)} async-done(((bf16[64,4,768]{2,1,0:T(4,128)(2,1)}), bf16[64,4,768]{2,1,0:T(4,128)(2,1)S(1)}, u32[]{:S(2)}, u32[]{:S(2)}) %all-to-all-start) | async-done | bytes 393248 | tf_op jit(solution)/shard_map/all_to_all | solution.py:68
  23.8 0.1 dynamic-slice_bitcast_fusion.1
  23.9 3.1 %collective-permute-start.2 = (bf16[4,1024]{1,0:T(4,128)(2,1)S(1)}, bf16[4,1024]{1,0:T(4,128)(2,1)S(1)}, u32[]{:S(2)}, u32[]{:S(2)}) collective-permute-start(bf16[4,1024]{1,0:T(4,128)(2,1)S(1)} %get-tuple-element.14), channel_id=1, source_target_pairs={{0,64},{64,128},{128,192},{192,0},{1,65},{65,129},{129,193},{193,1... | collective-permute-start | bytes 24584 | tf_op jit(solution)/shard_map/ppermute | solution.py:20
  27.0 4.2 %collective-permute-start.1 = (bf16[4,1024]{1,0:T(4,128)(2,1)S(1)}, bf16[4,1024]{1,0:T(4,128)(2,1)S(1)}, u32[]{:S(2)}, u32[]{:S(2)}) collective-permute-start(bf16[4,1024]{1,0:T(4,128)(2,1)S(1)} %get-tuple-element.15), channel_id=1, source_target_pairs={{0,128},{64,192},{128,0},{192,64},{1,129},{65,193},{129,1},{193,65... | collective-permute-start | bytes 24584 | tf_op jit(solution)/shard_map/ppermute | solution.py:20
  31.2 2.4 %collective-permute-start = (bf16[4,1024]{1,0:T(4,128)(2,1)S(1)}, bf16[4,1024]{1,0:T(4,128)(2,1)S(1)}, u32[]{:S(2)}, u32[]{:S(2)}) collective-permute-start(bf16[4,1024]{1,0:T(4,128)(2,1)S(1)} %get-tuple-element.16), channel_id=1, source_target_pairs={{0,192},{64,0},{128,64},{192,128},{1,193},{65,1},{129,65},{193,129... | collective-permute-start | bytes 24584 | tf_op jit(solution)/shard_map/ppermute | solution.py:20
  33.6 0.0 collective-permute-done.2
  33.6 0.0 collective-permute-done.1
  33.6 1.3 %collective-permute-done = bf16[4,1024]{1,0:T(4,128)(2,1)S(1)} collective-permute-done((bf16[4,1024]{1,0:T(4,128)(2,1)S(1)}, bf16[4,1024]{1,0:T(4,128)(2,1)S(1)}, u32[]{:S(2)}, u32[]{:S(2)}) %collective-permute-start) | collective-permute-done | bytes 8224 | tf_op jit(solution)/shard_map/ppermute | solution.py:20
  35.0 0.8 collective-permute-start.3
  35.8 2.0 %collective-permute-done.3 = bf16[4,4,1024]{2,1,0:T(4,128)(2,1)S(1)} collective-permute-done((bf16[4,4,1024]{2,1,0:T(4,128)(2,1)S(1)}, bf16[4,4,1024]{2,1,0:T(4,128)(2,1)S(1)}, u32[]{:S(2)}, u32[]{:S(2)}) %collective-permute-start.3) | collective-permute-done | bytes 32800 | tf_op jit(solution)/shard_map/ppermute | solution.py:24
  37.9 0.4 collective-permute-start.6
  38.3 2.3 %collective-permute-start.5 = (bf16[4,8,1024]{2,1,0:T(8,128)(2,1)S(1)}, bf16[4,8,1024]{2,1,0:T(8,128)(2,1)S(1)}, u32[]{:S(2)}, u32[]{:S(2)}) collective-permute-start(bf16[4,8,1024]{2,1,0:T(8,128)(2,1)S(1)} %pad_maximum_fusion.1), channel_id=1, source_target_pairs={{0,8},{4,12},{8,0},{12,4},{1,9},{5,13},{9,1},{13,5},{2,10},{6,14},... | collective-permute-start | bytes 196616 | tf_op jit(solution)/shard_map/ppermute | solution.py:20
  40.5 0.3 collective-permute-start.4
  40.9 2.1 %collective-permute-start.17 = (bf16[128,768]{1,0:T(8,128)(2,1)S(1)}, bf16[128,768]{1,0:T(8,128)(2,1)S(1)}, u32[]{:S(2)}, u32[]{:S(2)}) collective-permute-start(bf16[128,768]{1,0:T(8,128)(2,1)S(1)} %get-tuple-element.6), channel_id=1, source_target_pairs={{0,64},{64,128},{128,192},{192,0},{1,65},{65,129},{129,193},{193,1... | collective-permute-start | bytes 589832 | tf_op jit(solution)/shard_map/ppermute | solution.py:20
  43.0 1.6 %collective-permute-start.15 = (bf16[128,768]{1,0:T(8,128)(2,1)S(1)}, bf16[128,768]{1,0:T(8,128)(2,1)S(1)}, u32[]{:S(2)}, u32[]{:S(2)}) collective-permute-start(bf16[128,768]{1,0:T(8,128)(2,1)S(1)} %get-tuple-element.6), channel_id=1, source_target_pairs={{0,192},{64,0},{128,64},{192,128},{1,193},{65,1},{129,65},{193,129... | collective-permute-start | bytes 589832 | tf_op jit(solution)/shard_map/ppermute | solution.py:20
  44.6 0.0 collective-permute-done.6
  44.6 0.8 collective-permute-start.16
  45.4 0.0 collective-permute-done.5
  45.4 0.0 collective-permute-done.4
  45.4 0.1 select_select_fusion.3
  45.5 0.1 select_select_fusion.2
  45.6 0.2 collective-permute-start.9
  45.8 2.0 %collective-permute-start.8 = (bf16[4,32,1024]{2,1,0:T(8,128)(2,1)S(1)}, bf16[4,32,1024]{2,1,0:T(8,128)(2,1)S(1)}, u32[]{:S(2)}, u32[]{:S(2)}) collective-permute-start(bf16[4,32,1024]{2,1,0:T(8,128)(2,1)S(1)} %pad_maximum_fusion.refs_0_), channel_id=1, source_target_pairs={{0,32},{16,48},{32,0},{48,16},{1,33},{17,49},{33,1},{49,17},{2,34}... | collective-permute-start | bytes 786440 | tf_op jit(solution)/shard_map/ppermute | solution.py:20
  47.8 2.0 %collective-permute-done.17.prev_hi = bf16[128,768]{1,0:T(8,128)(2,1)S(1)} collective-permute-done((bf16[128,768]{1,0:T(8,128)(2,1)S(1)}, bf16[128,768]{1,0:T(8,128)(2,1)S(1)}, u32[]{:S(2)}, u32[]{:S(2)}) %collective-permute-start.17) | collective-permute-done | bytes 196640 | tf_op jit(solution)/shard_map/ppermute | solution.py:20
  49.8 0.9 %collective-permute-start.7 = (bf16[4,32,1024]{2,1,0:T(8,128)(2,1)S(1)}, bf16[4,32,1024]{2,1,0:T(8,128)(2,1)S(1)}, u32[]{:S(2)}, u32[]{:S(2)}) collective-permute-start(bf16[4,32,1024]{2,1,0:T(8,128)(2,1)S(1)} %pad_maximum_fusion.refs_0_), channel_id=1, source_target_pairs={{0,48},{16,0},{32,16},{48,32},{1,49},{17,1},{33,17},{49,33},{2,50}... | collective-permute-start | bytes 786440 | tf_op jit(solution)/shard_map/ppermute | solution.py:20
  50.7 0.1 collective-permute-done.15.next_hi
  50.8 2.5 %collective-permute-start.14 = (bf16[128,768]{1,0:T(8,128)(2,1)S(1)}, bf16[128,768]{1,0:T(8,128)(2,1)S(1)}, u32[]{:S(2)}, u32[]{:S(2)}) collective-permute-start(bf16[128,768]{1,0:T(8,128)(2,1)S(1)} %get-tuple-element.7), channel_id=1, source_target_pairs={{0,192},{64,0},{128,64},{192,128},{1,193},{65,1},{129,65},{193,129... | collective-permute-start | bytes 589832 | tf_op jit(solution)/shard_map/ppermute | solution.py:20
  53.3 4.0 %collective-permute-done.16.prev_lo = bf16[128,768]{1,0:T(8,128)(2,1)S(1)} collective-permute-done((bf16[128,768]{1,0:T(8,128)(2,1)S(1)}, bf16[128,768]{1,0:T(8,128)(2,1)S(1)}, u32[]{:S(2)}, u32[]{:S(2)}) %collective-permute-start.16) | collective-permute-done | bytes 196640 | tf_op jit(solution)/shard_map/ppermute | solution.py:20
  57.3 1.7 %collective-permute-start.19 = (bf16[128,768]{1,0:T(8,128)(2,1)S(1)}, bf16[128,768]{1,0:T(8,128)(2,1)S(1)}, u32[]{:S(2)}, u32[]{:S(2)}) collective-permute-start(bf16[128,768]{1,0:T(8,128)(2,1)S(1)} %collective-permute-done.17.prev_hi), channel_id=1, source_target_pairs={{0,64},{64,128},{128,192},{192,0},{1,65},{65,129},{129,193},{193,1... | collective-permute-start | bytes 589832 | tf_op jit(solution)/shard_map/ppermute | solution.py:20
  59.0 0.9 %collective-permute-done.14.next_lo = bf16[128,768]{1,0:T(8,128)(2,1)S(1)} collective-permute-done((bf16[128,768]{1,0:T(8,128)(2,1)S(1)}, bf16[128,768]{1,0:T(8,128)(2,1)S(1)}, u32[]{:S(2)}, u32[]{:S(2)}) %collective-permute-start.14) | collective-permute-done | bytes 196640 | tf_op jit(solution)/shard_map/ppermute | solution.py:20
  59.9 9.1 %collective-permute-start.10 = (bf16[4,32,1024]{2,1,0:T(8,128)(2,1)S(1)}, bf16[4,32,1024]{2,1,0:T(8,128)(2,1)S(1)}, u32[]{:S(2)}, u32[]{:S(2)}) collective-permute-start(bf16[4,32,1024]{2,1,0:T(8,128)(2,1)S(1)} %pad_maximum_fusion.refs_0_), channel_id=1, source_target_pairs={{0,1},{1,0},{2,3},{3,2},{4,5},{5,4},{6,7},{7,6},{8,9},{9,8},{10,11... | collective-permute-start | bytes 786440 | tf_op jit(solution)/shard_map/ppermute | solution.py:24
  69.0 0.0 collective-permute-done.9.refs_3_
  69.0 0.0 collective-permute-start.13
  69.0 0.5 collective-permute-start.12
  69.5 0.0 collective-permute-done.7.refs_1_
  69.5 0.1 collective-permute-start.11
  69.6 0.0 collective-permute-done.19.far_hi
  69.6 3.4 %collective-permute-start.18 = (bf16[128,768]{1,0:T(8,128)(2,1)S(1)}, bf16[128,768]{1,0:T(8,128)(2,1)S(1)}, u32[]{:S(2)}, u32[]{:S(2)}) collective-permute-start(bf16[128,768]{1,0:T(8,128)(2,1)S(1)} %collective-permute-done.14.next_lo), channel_id=1, source_target_pairs={{0,192},{64,0},{128,64},{192,128},{1,193},{65,1},{129,65},{193,129... | collective-permute-start | bytes 589832 | tf_op jit(solution)/shard_map/ppermute | solution.py:20
  73.0 0.2 copy.9.valid
  73.2 0.6 fusion.2
  74.5 0.1 pad_add_fusion.place
  74.6 6.5 %collective-permute-done.18.far_lo = bf16[128,768]{1,0:T(8,128)(2,1)S(1)} collective-permute-done((bf16[128,768]{1,0:T(8,128)(2,1)S(1)}, bf16[128,768]{1,0:T(8,128)(2,1)S(1)}, u32[]{:S(2)}, u32[]{:S(2)}) %collective-permute-start.18) | collective-permute-done | bytes 196640 | tf_op jit(solution)/shard_map/ppermute | solution.py:20
  81.1 1.8 %columns.1 = (bf16[2,4,4,32,768]{4,3,2,1,0:T(8,128)(2,1)S(1)}, bf16[2,4,4,32,768]{4,3,2,1,0:T(8,128)(2,1)S(1)}) custom-call(s32[2]{0:T(128)S(1)} %pad_add_fusion.place, bf16[256,768]{1,0:T(8,128)(2,1)S(1)} %copy-done, bf16[128,768]{1,0:T(8,128)(2,1)S(1)} %collective-permute-done.14.next_lo, bf16[128,768]{1,0:T(8,128)(2,1)S(1)} %collective-permute-done.15.next_hi, ...), custom_call_target="tpu_custom_call" | custom-call | flops 10000000 | bytes 6291456 | tf_op jit(solution)/shard_map/columns/pallas_call | solution.py:106
  83.0 0.0 collective-permute-done.13.refs_7_
  83.0 0.0 collective-permute-done.12.refs_6_
  83.0 6.5 %products.1 = (f32[1024,768]{1,0:T(8,128)}, f32[1024,768]{1,0:T(8,128)}) custom-call(f32[1]{0:T(128)} %bitcast.scale, bf16[4,32,1024]{2,1,0:T(8,128)(2,1)S(1)} %pad_maximum_fusion.refs_0_, bf16[4,32,1024]{2,1,0:T(8,128)(2,1)S(1)} %collective-permute-done.7.refs_1_, bf16[4,32,1024]{2,1,0:T(8,128)(2,1)S(1)} %collective-permute-done.8.refs_2_, ...), custom_call_target="tpu_custom_call" | custom-call | flops 3221225472 | bytes 12582912 | tf_op jit(solution)/shard_map/products/pallas_call | solution.py:119
  (20 shorter events, 0.4 us)
Async XLA Ops:
  0.6 40.2 %copy-start = (bf16[256,768]{1,0:T(8,128)(2,1)S(1)}, bf16[256,768]{1,0:T(8,128)(2,1)}, u32[]{:S(2)}) copy-start(bf16[256,768]{1,0:T(8,128)(2,1)} %own.1) | copy-start | bytes 1179652
  0.6 58.4 %copy-start.1 = (s32[1024]{0:T(1024)S(1)}, s32[1024]{0:T(1024)}, u32[]{:S(2)}) copy-start(s32[1024]{0:T(1024)} %param.4) | copy-start | bytes 12292
  2.5 21.1 %all-to-all-start = ((bf16[64,4,768]{2,1,0:T(4,128)(2,1)}), bf16[64,4,768]{2,1,0:T(4,128)(2,1)S(1)}, u32[]{:S(2)}, u32[]{:S(2)}) async-start(bf16[64,4,768]{2,1,0:T(4,128)(2,1)} %reshape.43), calls=%async_computation | async-start | bytes 786432 | tf_op jit(solution)/shard_map/all_to_all | solution.py:68
  23.9 9.7 %collective-permute-start.2 = (bf16[4,1024]{1,0:T(4,128)(2,1)S(1)}, bf16[4,1024]{1,0:T(4,128)(2,1)S(1)}, u32[]{:S(2)}, u32[]{:S(2)}) collective-permute-start(bf16[4,1024]{1,0:T(4,128)(2,1)S(1)} %get-tuple-element.14), channel_id=1, source_target_pairs={{0,64},{64,128},{128,192},{192,0},{1,65},{65,129},{129,193},{193,1... | collective-permute-start | bytes 24584 | tf_op jit(solution)/shard_map/ppermute | solution.py:20
  27.0 6.6 %collective-permute-start.1 = (bf16[4,1024]{1,0:T(4,128)(2,1)S(1)}, bf16[4,1024]{1,0:T(4,128)(2,1)S(1)}, u32[]{:S(2)}, u32[]{:S(2)}) collective-permute-start(bf16[4,1024]{1,0:T(4,128)(2,1)S(1)} %get-tuple-element.15), channel_id=1, source_target_pairs={{0,128},{64,192},{128,0},{192,64},{1,129},{65,193},{129,1},{193,65... | collective-permute-start | bytes 24584 | tf_op jit(solution)/shard_map/ppermute | solution.py:20
  31.2 3.7 %collective-permute-start = (bf16[4,1024]{1,0:T(4,128)(2,1)S(1)}, bf16[4,1024]{1,0:T(4,128)(2,1)S(1)}, u32[]{:S(2)}, u32[]{:S(2)}) collective-permute-start(bf16[4,1024]{1,0:T(4,128)(2,1)S(1)} %get-tuple-element.16), channel_id=1, source_target_pairs={{0,192},{64,0},{128,64},{192,128},{1,193},{65,1},{129,65},{193,129... | collective-permute-start | bytes 24584 | tf_op jit(solution)/shard_map/ppermute | solution.py:20
  35.0 2.9 %collective-permute-start.3 = (bf16[4,4,1024]{2,1,0:T(4,128)(2,1)S(1)}, bf16[4,4,1024]{2,1,0:T(4,128)(2,1)S(1)}, u32[]{:S(2)}, u32[]{:S(2)}) collective-permute-start(bf16[4,4,1024]{2,1,0:T(4,128)(2,1)S(1)} %pad_maximum_fusion.2), channel_id=1, source_target_pairs={{0,2},{2,0},{1,3},{3,1},{4,6},{6,4},{5,7},{7,5},{8,10},{10,8},{9,1... | collective-permute-start | bytes 98312 | tf_op jit(solution)/shard_map/ppermute | solution.py:24
  37.9 6.7 %collective-permute-start.6 = (bf16[4,8,1024]{2,1,0:T(8,128)(2,1)S(1)}, bf16[4,8,1024]{2,1,0:T(8,128)(2,1)S(1)}, u32[]{:S(2)}, u32[]{:S(2)}) collective-permute-start(bf16[4,8,1024]{2,1,0:T(8,128)(2,1)S(1)} %pad_maximum_fusion.1), channel_id=1, source_target_pairs={{0,4},{4,8},{8,12},{12,0},{1,5},{5,9},{9,13},{13,1},{2,6},{6,10},{... | collective-permute-start | bytes 196616 | tf_op jit(solution)/shard_map/ppermute | solution.py:20
  38.3 7.1 %collective-permute-start.5 = (bf16[4,8,1024]{2,1,0:T(8,128)(2,1)S(1)}, bf16[4,8,1024]{2,1,0:T(8,128)(2,1)S(1)}, u32[]{:S(2)}, u32[]{:S(2)}) collective-permute-start(bf16[4,8,1024]{2,1,0:T(8,128)(2,1)S(1)} %pad_maximum_fusion.1), channel_id=1, source_target_pairs={{0,8},{4,12},{8,0},{12,4},{1,9},{5,13},{9,1},{13,5},{2,10},{6,14},... | collective-permute-start | bytes 196616 | tf_op jit(solution)/shard_map/ppermute | solution.py:20
  40.5 4.9 %collective-permute-start.4 = (bf16[4,8,1024]{2,1,0:T(8,128)(2,1)S(1)}, bf16[4,8,1024]{2,1,0:T(8,128)(2,1)S(1)}, u32[]{:S(2)}, u32[]{:S(2)}) collective-permute-start(bf16[4,8,1024]{2,1,0:T(8,128)(2,1)S(1)} %pad_maximum_fusion.1), channel_id=1, source_target_pairs={{0,12},{4,0},{8,4},{12,8},{1,13},{5,1},{9,5},{13,9},{2,14},{6,2},{... | collective-permute-start | bytes 196616 | tf_op jit(solution)/shard_map/ppermute | solution.py:20
  40.9 8.9 %collective-permute-start.17 = (bf16[128,768]{1,0:T(8,128)(2,1)S(1)}, bf16[128,768]{1,0:T(8,128)(2,1)S(1)}, u32[]{:S(2)}, u32[]{:S(2)}) collective-permute-start(bf16[128,768]{1,0:T(8,128)(2,1)S(1)} %get-tuple-element.6), channel_id=1, source_target_pairs={{0,64},{64,128},{128,192},{192,0},{1,65},{65,129},{129,193},{193,1... | collective-permute-start | bytes 589832 | tf_op jit(solution)/shard_map/ppermute | solution.py:20
  43.0 7.8 %collective-permute-start.15 = (bf16[128,768]{1,0:T(8,128)(2,1)S(1)}, bf16[128,768]{1,0:T(8,128)(2,1)S(1)}, u32[]{:S(2)}, u32[]{:S(2)}) collective-permute-start(bf16[128,768]{1,0:T(8,128)(2,1)S(1)} %get-tuple-element.6), channel_id=1, source_target_pairs={{0,192},{64,0},{128,64},{192,128},{1,193},{65,1},{129,65},{193,129... | collective-permute-start | bytes 589832 | tf_op jit(solution)/shard_map/ppermute | solution.py:20
  44.6 12.7 %collective-permute-start.16 = (bf16[128,768]{1,0:T(8,128)(2,1)S(1)}, bf16[128,768]{1,0:T(8,128)(2,1)S(1)}, u32[]{:S(2)}, u32[]{:S(2)}) collective-permute-start(bf16[128,768]{1,0:T(8,128)(2,1)S(1)} %get-tuple-element.7), channel_id=1, source_target_pairs={{0,64},{64,128},{128,192},{192,0},{1,65},{65,129},{129,193},{193,1... | collective-permute-start | bytes 589832 | tf_op jit(solution)/shard_map/ppermute | solution.py:20
  45.6 23.4 %collective-permute-start.9 = (bf16[4,32,1024]{2,1,0:T(8,128)(2,1)S(1)}, bf16[4,32,1024]{2,1,0:T(8,128)(2,1)S(1)}, u32[]{:S(2)}, u32[]{:S(2)}) collective-permute-start(bf16[4,32,1024]{2,1,0:T(8,128)(2,1)S(1)} %pad_maximum_fusion.refs_0_), channel_id=1, source_target_pairs={{0,16},{16,32},{32,48},{48,0},{1,17},{17,33},{33,49},{49,1},{2,18}... | collective-permute-start | bytes 786440 | tf_op jit(solution)/shard_map/ppermute | solution.py:20
  45.8 23.2 %collective-permute-start.8 = (bf16[4,32,1024]{2,1,0:T(8,128)(2,1)S(1)}, bf16[4,32,1024]{2,1,0:T(8,128)(2,1)S(1)}, u32[]{:S(2)}, u32[]{:S(2)}) collective-permute-start(bf16[4,32,1024]{2,1,0:T(8,128)(2,1)S(1)} %pad_maximum_fusion.refs_0_), channel_id=1, source_target_pairs={{0,32},{16,48},{32,0},{48,16},{1,33},{17,49},{33,1},{49,17},{2,34}... | collective-permute-start | bytes 786440 | tf_op jit(solution)/shard_map/ppermute | solution.py:20
  49.8 19.7 %collective-permute-start.7 = (bf16[4,32,1024]{2,1,0:T(8,128)(2,1)S(1)}, bf16[4,32,1024]{2,1,0:T(8,128)(2,1)S(1)}, u32[]{:S(2)}, u32[]{:S(2)}) collective-permute-start(bf16[4,32,1024]{2,1,0:T(8,128)(2,1)S(1)} %pad_maximum_fusion.refs_0_), channel_id=1, source_target_pairs={{0,48},{16,0},{32,16},{48,32},{1,49},{17,1},{33,17},{49,33},{2,50}... | collective-permute-start | bytes 786440 | tf_op jit(solution)/shard_map/ppermute | solution.py:20
  50.8 9.1 %collective-permute-start.14 = (bf16[128,768]{1,0:T(8,128)(2,1)S(1)}, bf16[128,768]{1,0:T(8,128)(2,1)S(1)}, u32[]{:S(2)}, u32[]{:S(2)}) collective-permute-start(bf16[128,768]{1,0:T(8,128)(2,1)S(1)} %get-tuple-element.7), channel_id=1, source_target_pairs={{0,192},{64,0},{128,64},{192,128},{1,193},{65,1},{129,65},{193,129... | collective-permute-start | bytes 589832 | tf_op jit(solution)/shard_map/ppermute | solution.py:20
  57.3 12.3 %collective-permute-start.19 = (bf16[128,768]{1,0:T(8,128)(2,1)S(1)}, bf16[128,768]{1,0:T(8,128)(2,1)S(1)}, u32[]{:S(2)}, u32[]{:S(2)}) collective-permute-start(bf16[128,768]{1,0:T(8,128)(2,1)S(1)} %collective-permute-done.17.prev_hi), channel_id=1, source_target_pairs={{0,64},{64,128},{128,192},{192,0},{1,65},{65,129},{129,193},{193,1... | collective-permute-start | bytes 589832 | tf_op jit(solution)/shard_map/ppermute | solution.py:20
  59.9 23.0 %collective-permute-start.10 = (bf16[4,32,1024]{2,1,0:T(8,128)(2,1)S(1)}, bf16[4,32,1024]{2,1,0:T(8,128)(2,1)S(1)}, u32[]{:S(2)}, u32[]{:S(2)}) collective-permute-start(bf16[4,32,1024]{2,1,0:T(8,128)(2,1)S(1)} %pad_maximum_fusion.refs_0_), channel_id=1, source_target_pairs={{0,1},{1,0},{2,3},{3,2},{4,5},{5,4},{6,7},{7,6},{8,9},{9,8},{10,11... | collective-permute-start | bytes 786440 | tf_op jit(solution)/shard_map/ppermute | solution.py:24
  69.0 14.0 %collective-permute-start.13 = (bf16[4,32,1024]{2,1,0:T(8,128)(2,1)S(1)}, bf16[4,32,1024]{2,1,0:T(8,128)(2,1)}, u32[]{:S(2)}, u32[]{:S(2)}) collective-permute-start(bf16[4,32,1024]{2,1,0:T(8,128)(2,1)S(1)} %collective-permute-done.9.refs_3_), channel_id=1, source_target_pairs={{0,1},{1,0},{2,3},{3,2},{4,5},{5,4},{6,7},{7,6},{8,9},{9,8},{10,11... | collective-permute-start | bytes 786440 | tf_op jit(solution)/shard_map/ppermute | solution.py:24
  69.0 14.0 %collective-permute-start.12 = (bf16[4,32,1024]{2,1,0:T(8,128)(2,1)S(1)}, bf16[4,32,1024]{2,1,0:T(8,128)(2,1)}, u32[]{:S(2)}, u32[]{:S(2)}) collective-permute-start(bf16[4,32,1024]{2,1,0:T(8,128)(2,1)S(1)} %collective-permute-done.8.refs_2_), channel_id=1, source_target_pairs={{0,1},{1,0},{2,3},{3,2},{4,5},{5,4},{6,7},{7,6},{8,9},{9,8},{10,11... | collective-permute-start | bytes 786440 | tf_op jit(solution)/shard_map/ppermute | solution.py:24
  69.5 13.5 %collective-permute-start.11 = (bf16[4,32,1024]{2,1,0:T(8,128)(2,1)S(1)}, bf16[4,32,1024]{2,1,0:T(8,128)(2,1)}, u32[]{:S(2)}, u32[]{:S(2)}) collective-permute-start(bf16[4,32,1024]{2,1,0:T(8,128)(2,1)S(1)} %collective-permute-done.7.refs_1_), channel_id=1, source_target_pairs={{0,1},{1,0},{2,3},{3,2},{4,5},{5,4},{6,7},{7,6},{8,9},{9,8},{10,11... | collective-permute-start | bytes 786440 | tf_op jit(solution)/shard_map/ppermute | solution.py:24
  69.6 11.5 %collective-permute-start.18 = (bf16[128,768]{1,0:T(8,128)(2,1)S(1)}, bf16[128,768]{1,0:T(8,128)(2,1)S(1)}, u32[]{:S(2)}, u32[]{:S(2)}) collective-permute-start(bf16[128,768]{1,0:T(8,128)(2,1)S(1)} %collective-permute-done.14.next_lo), channel_id=1, source_target_pairs={{0,192},{64,0},{128,64},{192,128},{1,193},{65,1},{129,65},{193,129... | collective-permute-start | bytes 589832 | tf_op jit(solution)/shard_map/ppermute | solution.py:20

commit v2 on v0

v2 whole, which is shorter than its diff:
```python
import functools

import jax
import jax.numpy as jnp
from jax import lax
from jax.experimental import pallas as pl
from jax.experimental.pallas import tpu as pltpu
from jax.sharding import Mesh, PartitionSpec as P

S = 4096
LAG = 256
FRAMES = 1024
W = 768
ROWS = 1024
HALF = 512
AXES = ("tm", "y", "x", "zl", "core")
TILE = ("y", "x", "zl", "core")
F32 = jnp.float32
BF16 = jnp.bfloat16


def shift(value, axis, size, step):
    return lax.ppermute(value, axis, [(i, (i + step) % size) for i in range(size)])


def swap(value, axis):
    return lax.ppermute(value, axis, [(0, 1), (1, 0)])


def columns_kernel(tm, own, next_, prev, far_lo, far_hi, valid, out, sums, held, sems):
    parts = ((own, held.at[0]), (next_, held.at[1]), (prev, held.at[3]), (far_lo, held.at[2, :128]), (far_hi, held.at[2, 128:]))
    copies = [pltpu.make_async_copy(a, b, sems.at[n]) for n, (a, b) in enumerate(parts)]
    for copy in copies:
        copy.start()
    for copy in copies:
        copy.wait()
    total = jnp.zeros((1, W), F32)
    for d in range(4):
        total += jnp.sum(held[d].astype(F32), axis=0, keepdims=True)
    mean = total * (1.0 / FRAMES)
    for d in range(4):
        held[d] = (held[d].astype(F32) - mean).astype(BF16)
    c_total = jnp.zeros((1, W), F32)
    r_total = jnp.zeros((1, W), F32)
    for d in range(4):
        j = lax.rem(tm[0] + d, 4)
        i = lax.rem(tm[0] + d + 3, 4)
        here = held[d]
        out[:, d, :, :W] = here.reshape(16, 16, W)
        c_total += jnp.sum(here.astype(F32), axis=0, keepdims=True)
        here = held[(d + 1) % 4].astype(F32) * valid[j] + held[(d + 3) % 4].astype(F32) * valid[i]
        here = here.astype(BF16)
        out[:, d, :, W:] = here.reshape(16, 16, W)
        r_total += jnp.sum(here.astype(F32), axis=0, keepdims=True)
    sums[:, :W] = c_total
    sums[:, W:] = r_total


def product_kernel(which, scale, slab, right, sums, *refs):
    instant, lagged = refs[-2:]
    left = slab[...].T
    mean = jnp.sum(left.astype(F32), axis=1, keepdims=True) * (1.0 / FRAMES)
    value = jnp.dot(left, right[:, :W], preferred_element_type=F32)
    instant[...] = (value - mean * sums[:, :W]) * (1.0 / FRAMES)
    value = jnp.dot(left, right[:, W:], preferred_element_type=F32)
    lagged[...] = (value - mean * sums[:, W:]) * scale[0]


def products(which, scale, slab, right, sums, before=()):
    tile = 256
    steps = HALF // tile
    return pl.pallas_call(
        product_kernel,
        grid_spec=pltpu.PrefetchScalarGridSpec(
            num_scalar_prefetch=1,
            grid=(steps,),
            in_specs=[pl.BlockSpec(memory_space=pltpu.SMEM)]
            + [pl.BlockSpec((FRAMES, tile), lambda i, w: (0, i))]
            + [pl.BlockSpec((FRAMES, 2 * W), lambda i, w: (0, 0))]
            + [pl.BlockSpec((1, 2 * W), lambda i, w: (0, 0))]
            + [pl.BlockSpec(memory_space=pl.ANY)] * len(before),
            out_specs=[pl.BlockSpec((tile, W), lambda i, w: (w[0] * steps + i, 0))] * 2,
        ),
        out_shape=[jax.ShapeDtypeStruct((ROWS, W), F32)] * 2,
        input_output_aliases={5: 0, 6: 1} if before else {},
        compiler_params=pltpu.CompilerParams(vmem_limit_bytes=20 * 2**20),
        cost_estimate=pl.CostEstimate(flops=4 * FRAMES * HALF * W, bytes_accessed=6 * 2**20, transcendentals=0),
        name="products",
    )(which, scale, slab, right, sums, *before)


def shards(frames, segments, offset):
    tm = lax.axis_index("tm")
    zl, core = lax.axis_index("zl"), lax.axis_index("core")
    start = offset[0]

    prev = shift(frames, "tm", 4, 1)
    next_ = shift(frames, "tm", 4, -1)

    blocks = segments.reshape(4, LAG)
    valid = jnp.concatenate([blocks[:3] == blocks[1:], jnp.zeros((1, LAG), jnp.bool_)]).astype(F32)
    scale = (0.5 / jnp.sum(valid)).reshape(1)
    valid = valid[:, :, None]
    place = tm.reshape(1)
    def pick(frames):
        spread = lax.all_to_all(frames.reshape(16, 16, W), ("y", "x"), 0, 0, tiled=True)
        first = jnp.minimum(start // (4 * W), 13)
        mine = lax.dynamic_slice(spread, (first, 0, 0), (3, 16, W))
        column = zl * 2 + core
        zero = jnp.zeros((16, W), BF16)
        row = []
        for p in range(3):
            row += [jnp.where(column == n, mine[p], zero) for n in range(4)]
        row = lax.dynamic_slice(jnp.concatenate(row, axis=1), (0, start - first * 4 * W), (16, S))
        row = row.reshape(16, 4, 2, HALF)
        even = core == 0
        keep = jnp.where(even, row[:, :, 0], row[:, :, 1])
        give = jnp.where(even, row[:, :, 1], row[:, :, 0])
        return keep + swap(give, "core")

    keep = lax.cond(start >= 0, pick, lambda frames: jnp.zeros((16, 4, HALF), BF16), frames)
    keep, prev, next_ = lax.optimization_barrier((keep, prev, next_))
    keep = keep + swap(keep, "zl")

    def block(d):
        return lax.dynamic_slice(keep, (0, lax.rem(tm + d, 4), 0), (16, 1, HALF)).reshape(16, HALF)

    got = {d: shift(block(4 - d), "tm", 4, 4 - d) for d in (2, 1, 3)}
    part = jnp.stack([block(0), got[1], got[2], got[3]])
    part, prev, next_, scale, valid, place = lax.optimization_barrier((part, prev, next_, scale, valid, place))
    far_hi = shift(prev[128:], "tm", 4, 1)
    far_lo = shift(next_[:128], "tm", 4, -1)
    part = jnp.broadcast_to(part.reshape(1, 64, HALF), (16, 64, HALF))
    own = lax.all_to_all(part, ("y", "x"), 0, 0, tiled=True).reshape(FRAMES, HALF)

    smem = pl.BlockSpec(memory_space=pltpu.SMEM)
    vmem = pl.BlockSpec(memory_space=pltpu.VMEM)
    right, sums = pl.pallas_call(
        columns_kernel,
        out_shape=[jax.ShapeDtypeStruct((16, 4, 16, 2 * W), BF16), jax.ShapeDtypeStruct((1, 2 * W), F32)],
        in_specs=[smem] + [pl.BlockSpec(memory_space=pltpu.HBM)] * 5 + [vmem],
        out_specs=[vmem] * 2,
        scratch_shapes=[pltpu.VMEM((4, LAG, W), BF16), pltpu.SemaphoreType.DMA((5,))],
        compiler_params=pltpu.CompilerParams(vmem_limit_bytes=16 * 2**20),
        cost_estimate=pl.CostEstimate(flops=10**7, bytes_accessed=6 * 2**20, transcendentals=0),
        name="columns",
    )(place, frames, next_, prev, far_lo, far_hi, valid)
    own, right, sums = lax.optimization_barrier((own, right, sums))
    other = swap(own, "core")
    right = right.reshape(FRAMES, 2 * W)

    outs = products(core.reshape(1), scale, own, right, sums)
    outs = products(1 - core.reshape(1), scale, other, right, sums, outs)
    return tuple(outs)


def solution(mesh):
    fine = Mesh(mesh.devices.reshape(4, 4, 4, 2, 2), AXES)
    cut = P("tm", TILE)
    return jax.shard_map(shards, mesh=fine, in_specs=(cut, P(), P()), out_specs=(cut, cut), check_vma=False)
```

time: 674 us -> 76.2 us (0.11)
  waiting for transfers between devices: 615 us -> 12.9 us
  starting transfers between devices: 5.98 us -> 38.3 us
  between operations: 16.3 us -> 2.11 us
  other arithmetic: 12.4 us -> 1.94 us
  Pallas kernels: 0 us -> 9.84 us
  matrix products: 8.43 us -> 0 us
  local copies, waits for them, and re-layouts: 15.1 us -> 7.67 us
    psum x1 -> x0, waiting for transfers between devices: 573 us -> none  [broadcast(): return lax.psum(jnp.where(mine, value, jnp.zeros_like(value)), axis)]
    all_to_all x1 -> x2, waiting for transfers between devices: 40.9 us -> 6.25 us  [the longest x1 6.24 us: pick(): lax.all_to_all(frames.reshape(16, 16, W), ('y', 'x'), 0, 0, tiled=True)]
    ppermute x0 -> x10, starting transfers between devices: none -> 26.1 us  [the longest x7 18.7 us: shift(): lax.ppermute(value, axis, [(i, (i + step) % size) for i in range(size)])]
    pallas_call x0 -> x3, Pallas kernels: none -> 9.84 us  [the longest x2 7.13 us: products(): pl.pallas_call(product_kernel, grid_spec=pltpu.PrefetchScalarGridSpec(num...]
    dot_general x2 -> x0, matrix products: 8.43 us -> none  [the longest x1 4.9 us: shards(): lax.dot_general(left, right, dims, preferred_element_type=jnp.float32) * 0.5]
    convert_element_type x3 -> x0, other arithmetic: 6.9 us -> none  [center(): return (values.astype(jnp.float32) - mean).astype(jnp.bfloat16)]
  transfers between devices with their start and end apart: 3 -> 12, of which waited for: 2 -> 4; matrix products, arithmetic and copies ran while one was open for 2% -> 4% of each run, Pallas kernels for 0% -> 9%
where the time goes in v2:
time: 76.2 us; the launch traced here: 75.6 us
  starting transfers between devices  38.3 us (50%)
  waiting for transfers between devices  12.9 us (17%)
  Pallas kernels  9.84 us (13%)
  local copies, waits for them, and re-layouts  7.67 us (10%)
  loops' own time  2.78 us (4%)
  between operations  2.11 us (3%)
  other arithmetic  1.94 us (3%)
    ppermute x7, starting transfers between devices, shift(): lax.ppermute(value, axis, [(i, (i + step) % size) for i in range(size)])  18.7 us
    ppermute x3, starting transfers between devices, swap(): return lax.ppermute(value, axis, [(0, 1), (1, 0)])  7.43 us
    pallas_call x2, Pallas kernels, products(): pl.pallas_call(product_kernel, grid_spec=pltpu.PrefetchScalarGridSpec(num...  7.13 us
    all_to_all x1, starting transfers between devices, pick(): lax.all_to_all(frames.reshape(16, 16, W), ('y', 'x'), 0, 0, tiled=True)  6.77 us
    all_to_all x1, waiting for transfers between devices, pick(): lax.all_to_all(frames.reshape(16, 16, W), ('y', 'x'), 0, 0, tiled=True)  6.24 us
    all_to_all x1, starting transfers between devices, shards(): lax.all_to_all(part, ('y', 'x'), 0, 0, tiled=True).reshape(FRAMES, HALF)  5.41 us
    unnamed x14, local copies, waits for them, and re-layouts  5.28 us
    ppermute x7, waiting for transfers between devices, shift(): lax.ppermute(value, axis, [(i, (i + step) % size) for i in range(size)])  4.18 us
  transfers between devices with their start and end apart: 12, of which 4 were waited for; matrix products, arithmetic and copies ran while one was open for 4% of the time, Pallas kernels for 9%

profile of v2, /device:TPU:1, one launch (start us, length us, event | category | flops | bytes accessed | tf_op | source)
XLA Modules:
  0.0 75.6 jit_solution(819710365095524515)
XLA Ops:
  0.6 3.9 %collective-permute-start.1 = (bf16[256,768]{1,0:T(8,128)(2,1)}, bf16[256,768]{1,0:T(8,128)(2,1)S(1)}, u32[]{:S(2)}, u32[]{:S(2)}) collective-permute-start(bf16[256,768]{1,0:T(8,128)(2,1)} %own.1), channel_id=1, source_target_pairs={{0,64},{64,128},{128,192},{192,0},{1,65},{65,129},{129,193},{193,1... | collective-permute-start | bytes 1179656 | tf_op jit(solution)/shard_map/ppermute | solution.py:23
  4.5 3.1 %collective-permute-start.2 = (bf16[256,768]{1,0:T(8,128)(2,1)}, bf16[256,768]{1,0:T(8,128)(2,1)S(1)}, u32[]{:S(2)}, u32[]{:S(2)}) collective-permute-start(bf16[256,768]{1,0:T(8,128)(2,1)} %own.1), channel_id=1, source_target_pairs={{0,192},{64,0},{128,64},{192,128},{1,193},{65,1},{129,65},{193,129... | collective-permute-start | bytes 1179656 | tf_op jit(solution)/shard_map/ppermute | solution.py:23
  8.3 19.7 %conditional.1 = (bf16[16,4,512]{2,0,1:T(8,128)(2,1)S(1)}) conditional(s32[]{:T(128)} %convert_element_type.6, () %tuple.16, (s32[]{:T(128)}, s32[]{:T(128)}, bf16[256,768]{1,0:T(8,128)(2,1)}, s32[]{:T(128)}) %tuple.17), branch_computations={%region_0.0_spmd, %region_1.0_spmd} | conditional | flops 245785 | bytes 3146148 | solution.py:121
  8.3 6.8 %all-to-all-start = ((bf16[16,16,768]{2,1,0:T(8,128)(2,1)}), bf16[16,16,768]{2,1,0:T(8,128)(2,1)S(1)}, u32[]{:S(2)}, u32[]{:S(2)}) async-start(bf16[16,16,768]{2,1,0:T(8,128)(2,1)} %bitcast.53), calls=%async_computation | async-start | bytes 786432 | tf_op jit(solution)/shard_map/cond/branch_1_fun/all_to_all | solution.py:106
  17.7 6.2 %all-to-all-done = bf16[16,16,768]{2,1,0:T(8,128)(2,1)S(1)} async-done(((bf16[16,16,768]{2,1,0:T(8,128)(2,1)}), bf16[16,16,768]{2,1,0:T(8,128)(2,1)S(1)}, u32[]{:S(2)}, u32[]{:S(2)}) %all-to-all-start) | async-done | bytes 393248 | tf_op jit(solution)/shard_map/cond/branch_1_fun/all_to_all | solution.py:106
  24.2 0.1 constant_dynamic-slice_fusion
  24.4 0.1 reshape.88
  24.4 0.3 broadcast_select_fusion.1
  24.8 2.2 %collective-permute-start = (bf16[16,4,512]{2,0,1:T(8,128)(2,1)S(1)}, bf16[16,4,512]{2,0,1:T(8,128)(2,1)S(1)}, u32[]{:S(2)}, u32[]{:S(2)}) collective-permute-start(bf16[16,4,512]{2,0,1:T(8,128)(2,1)S(1)} %bitcast.55), channel_id=1, source_target_pairs={{0,1},{1,0},{2,3},{3,2},{4,5},{5,4},{6,7},{7,6},{8,9},{9,8},{10,11... | collective-permute-start | bytes 196616 | tf_op jit(solution)/shard_map/cond/branch_1_fun/ppermute | solution.py:27
  27.1 0.9 %collective-permute-done = bf16[16,4,512]{2,0,1:T(8,128)(2,1)S(1)} collective-permute-done((bf16[16,4,512]{2,0,1:T(8,128)(2,1)S(1)}, bf16[16,4,512]{2,0,1:T(8,128)(2,1)S(1)}, u32[]{:S(2)}, u32[]{:S(2)}) %collective-permute-start) | collective-permute-done | bytes 65568 | tf_op jit(solution)/shard_map/cond/branch_1_fun/ppermute | solution.py:27
  28.0 0.0 collective-permute-done.1.prev
  28.0 0.0 collective-permute-done.2.next_
  28.0 0.0 copy-start.1
  28.0 0.8 %collective-permute-start.3 = (bf16[16,4,512]{2,0,1:T(8,128)(2,1)S(1)}, bf16[16,4,512]{2,0,1:T(8,128)(2,1)S(1)}, u32[]{:S(2)}, u32[]{:S(2)}) collective-permute-start(bf16[16,4,512]{2,0,1:T(8,128)(2,1)S(1)} %get-tuple-element.55), channel_id=1, source_target_pairs={{0,2},{2,0},{1,3},{3,1},{4,6},{6,4},{5,7},{7,5},{8,10},{10,8},{9,1... | collective-permute-start | bytes 196616 | tf_op jit(solution)/shard_map/ppermute | solution.py:27
  28.9 0.8 %slice_compare_fusion = pred[768]{0:T(1024)(128)(4,1)S(1)} fusion(s32[1024]{0:T(1024)} %param.6), kind=kLoop, calls=%fused_computation.24 | loop fusion | flops 768 | bytes 6912 | tf_op jit(solution)/shard_map/eq | solution.py:101
  29.7 1.6 %collective-permute-done.3 = bf16[16,4,512]{2,0,1:T(8,128)(2,1)S(1)} collective-permute-done((bf16[16,4,512]{2,0,1:T(8,128)(2,1)S(1)}, bf16[16,4,512]{2,0,1:T(8,128)(2,1)S(1)}, u32[]{:S(2)}, u32[]{:S(2)}) %collective-permute-start.3) | collective-permute-done | bytes 65568 | tf_op jit(solution)/shard_map/ppermute | solution.py:27
  31.3 1.5 %collective-permute-start.6 = (bf16[16,512]{1,0:T(8,128)(2,1)S(1)}, bf16[16,512]{1,0:T(8,128)(2,1)S(1)}, u32[]{:S(2)}, u32[]{:S(2)}) collective-permute-start(bf16[16,512]{1,0:T(8,128)(2,1)S(1)} %get-tuple-element.52), channel_id=1, source_target_pairs={{0,64},{64,128},{128,192},{192,0},{1,65},{65,129},{129,193},{193,1... | collective-permute-start | bytes 49160 | tf_op jit(solution)/shard_map/ppermute | solution.py:23
  32.8 3.1 %collective-permute-start.5 = (bf16[16,512]{1,0:T(8,128)(2,1)S(1)}, bf16[16,512]{1,0:T(8,128)(2,1)S(1)}, u32[]{:S(2)}, u32[]{:S(2)}) collective-permute-start(bf16[16,512]{1,0:T(8,128)(2,1)S(1)} %get-tuple-element.53), channel_id=1, source_target_pairs={{0,128},{64,192},{128,0},{192,64},{1,129},{65,193},{129,1},{193,65... | collective-permute-start | bytes 49160 | tf_op jit(solution)/shard_map/ppermute | solution.py:23
  35.8 3.5 %collective-permute-start.4 = (bf16[16,512]{1,0:T(8,128)(2,1)S(1)}, bf16[16,512]{1,0:T(8,128)(2,1)S(1)}, u32[]{:S(2)}, u32[]{:S(2)}) collective-permute-start(bf16[16,512]{1,0:T(8,128)(2,1)S(1)} %get-tuple-element.54), channel_id=1, source_target_pairs={{0,192},{64,0},{128,64},{192,128},{1,193},{65,1},{129,65},{193,129... | collective-permute-start | bytes 49160 | tf_op jit(solution)/shard_map/ppermute | solution.py:23
  39.3 0.6 convert_reduce_fusion
  40.6 0.0 collective-permute-done.6
  40.6 0.0 collective-permute-done.5
  40.6 0.0 collective-permute-done.4
  40.7 1.1 %broadcast_in_dim.13 = bf16[16,64,512]{2,1,0:T(8,128)(2,1)} broadcast(bf16[64,512]{1,0:T(8,128)(2,1)S(1)} %bitcast.54), dimensions={1,2} | broadcast | bytes 1114112 | tf_op jit(solution)/shard_map/broadcast_in_dim | solution.py:133
  41.7 5.4 %all-to-all-start.1 = ((bf16[16,64,512]{2,1,0:T(8,128)(2,1)}), bf16[16,64,512]{2,1,0:T(8,128)(2,1)}, u32[]{:S(2)}, u32[]{:S(2)}) async-start(bf16[16,64,512]{2,1,0:T(8,128)(2,1)} %broadcast_in_dim.13), calls=%async_computation.1 | async-start | bytes 2097152 | tf_op jit(solution)/shard_map/all_to_all | solution.py:134
  47.2 0.9 %collective-permute-start.8 = (bf16[128,768]{1,0:T(8,128)(2,1)S(1)}, bf16[128,768]{1,0:T(8,128)(2,1)S(1)}, u32[]{:S(2)}, u32[]{:S(2)}) collective-permute-start(bf16[128,768]{1,0:T(8,128)(2,1)S(1)} %slice.59), channel_id=1, source_target_pairs={{0,64},{64,128},{128,192},{192,0},{1,65},{65,129},{129,193},{193,1... | collective-permute-start | bytes 589832 | tf_op jit(solution)/shard_map/ppermute | solution.py:23
  48.1 2.7 %collective-permute-start.7 = (bf16[128,768]{1,0:T(8,128)(2,1)S(1)}, bf16[128,768]{1,0:T(8,128)(2,1)S(1)}, u32[]{:S(2)}, u32[]{:S(2)}) collective-permute-start(bf16[128,768]{1,0:T(8,128)(2,1)S(1)} %slice.58), channel_id=1, source_target_pairs={{0,192},{64,0},{128,64},{192,128},{1,193},{65,1},{129,65},{193,129... | collective-permute-start | bytes 589832 | tf_op jit(solution)/shard_map/ppermute | solution.py:23
  50.9 1.0 %copy.21.valid = f32[4,256,1]{2,1,0:T(8,128)} copy(f32[4,256,1]{1,0,2:T(4,128)S(1)} %convert_bitcast_fusion) | data formatting | bytes 8192 | tf_op jit(solution)/shard_map/optimization_barrier | solution.py:130
  51.9 4.2 %collective-permute-done.8.far_hi = bf16[128,768]{1,0:T(8,128)(2,1)S(1)} collective-permute-done((bf16[128,768]{1,0:T(8,128)(2,1)S(1)}, bf16[128,768]{1,0:T(8,128)(2,1)S(1)}, u32[]{:S(2)}, u32[]{:S(2)}) %collective-permute-start.8) | collective-permute-done | bytes 196640 | tf_op jit(solution)/shard_map/ppermute | solution.py:23
  56.0 0.0 copy-done.1
  56.1 0.0 copy-start.3
  56.1 0.7 copy-done.3
  56.7 0.0 collective-permute-done.7.far_lo
  56.8 0.0 copy-start.5
  56.8 0.7 copy-done.5
  57.4 0.0 copy-start
  57.4 1.0 %copy-done = f32[4,256,1]{2,1,0:T(8,128)S(1)} copy-done((f32[4,256,1]{2,1,0:T(8,128)S(1)}, f32[4,256,1]{2,1,0:T(8,128)}, u32[]{:S(2)}) %copy-start) | copy-done | bytes 4120
  58.5 0.0 copy-start.2
  58.5 1.0 %copy-done.2 = bf16[256,768]{1,0:T(8,128)(2,1)S(1)} copy-done((bf16[256,768]{1,0:T(8,128)(2,1)S(1)}, bf16[256,768]{1,0:T(8,128)(2,1)}, u32[]{:S(2)}) %copy-start.2) | copy-done | bytes 393240
  59.5 0.0 copy-start.4
  59.5 0.9 %copy-done.4 = bf16[128,768]{1,0:T(8,128)(2,1)S(1)} copy-done((bf16[128,768]{1,0:T(8,128)(2,1)S(1)}, bf16[128,768]{1,0:T(8,128)(2,1)}, u32[]{:S(2)}) %copy-start.4) | copy-done | bytes 196632
  60.4 0.9 %copy-done.6 = bf16[128,768]{1,0:T(8,128)(2,1)S(1)} copy-done((bf16[128,768]{1,0:T(8,128)(2,1)S(1)}, bf16[128,768]{1,0:T(8,128)(2,1)}, u32[]{:S(2)}) %copy-start.6) | copy-done | bytes 196632
  61.3 2.7 %columns.1 = (bf16[16,4,16,1536]{3,2,1,0:T(8,128)(2,1)S(1)}, f32[1,1536]{1,0:T(1,128)S(1)}) custom-call(s32[1]{0:T(128)} %bitcast.26.tm, bf16[256,768]{1,0:T(8,128)(2,1)} %own.1, bf16[256,768]{1,0:T(8,128)(2,1)S(1)} %copy-done.2, bf16[256,768]{1,0:T(8,128)(2,1)S(1)} %collective-permute-done.1.prev, bf16[128,768]{1,0:T(8,128)(2,1)S(1)} %copy-done.6, ...), custom_call_target="tpu_custom_call" | custom-call | flops 10000000 | bytes 6291456 | tf_op jit(solution)/shard_map/columns/pallas_call | solution.py:138
  64.1 0.0 all-to-all-done.1
  64.1 4.4 %collective-permute-start.9 = (bf16[1024,512]{1,0:T(8,128)(2,1)}, bf16[1024,512]{1,0:T(8,128)(2,1)S(1)}, u32[]{:S(2)}, u32[]{:S(2)}) collective-permute-start(bf16[1024,512]{1,0:T(8,128)(2,1)} %bitcast.28.slab), channel_id=1, source_target_pairs={{0,1},{1,0},{2,3},{3,2},{4,5},{5,4},{6,7},{7,6},{8,9},{9,8},{10,11... | collective-permute-start | bytes 3145736 | tf_op jit(solution)/shard_map/ppermute | solution.py:27
  68.4 4.0 %products.2 = (f32[1024,768]{1,0:T(8,128)}, f32[1024,768]{1,0:T(8,128)}) custom-call(s32[1]{0:T(128)} %bitcast.15.which, f32[1]{0:T(128)} %bitcast.24.scale, bf16[1024,512]{1,0:T(8,128)(2,1)} %bitcast.28.slab, bf16[1024,1536]{1,0:T(8,128)(2,1)S(1)} %bitcast.51, f32[1,1536]{1,0:T(1,128)S(1)} %get-tuple-element.46.sums), custom_call_target="tpu_custom_call" | custom-call | flops 1610612736 | bytes 6291456 | tf_op jit(solution)/shard_map/products/pallas_call | solution.py:72
  72.5 0.0 collective-permute-done.9.slab
  72.5 3.1 %products.3 = (f32[1024,768]{1,0:T(8,128)}, f32[1024,768]{1,0:T(8,128)}) custom-call(s32[1]{0:T(128)S(6)} %sub.10.which, f32[1]{0:T(128)} %bitcast.24.scale, bf16[1024,512]{1,0:T(8,128)(2,1)S(1)} %collective-permute-done.9.slab, bf16[1024,1536]{1,0:T(8,128)(2,1)S(1)} %bitcast.52, ...), custom_call_target="tpu_custom_call", output_to_operand_aliasing={{0}: (5, {}), {1}: (6, {})} | custom-call | flops 1610612736 | bytes 6291456 | tf_op jit(solution)/shard_map/products/pallas_call | solution.py:72
  (22 shorter events, 0.4 us)
Async XLA Ops:
  0.6 27.4 %collective-permute-start.1 = (bf16[256,768]{1,0:T(8,128)(2,1)}, bf16[256,768]{1,0:T(8,128)(2,1)S(1)}, u32[]{:S(2)}, u32[]{:S(2)}) collective-permute-start(bf16[256,768]{1,0:T(8,128)(2,1)} %own.1), channel_id=1, source_target_pairs={{0,64},{64,128},{128,192},{192,0},{1,65},{65,129},{129,193},{193,1... | collective-permute-start | bytes 1179656 | tf_op jit(solution)/shard_map/ppermute | solution.py:23
  4.5 23.5 %collective-permute-start.2 = (bf16[256,768]{1,0:T(8,128)(2,1)}, bf16[256,768]{1,0:T(8,128)(2,1)S(1)}, u32[]{:S(2)}, u32[]{:S(2)}) collective-permute-start(bf16[256,768]{1,0:T(8,128)(2,1)} %own.1), channel_id=1, source_target_pairs={{0,192},{64,0},{128,64},{192,128},{1,193},{65,1},{129,65},{193,129... | collective-permute-start | bytes 1179656 | tf_op jit(solution)/shard_map/ppermute | solution.py:23
  8.3 15.7 %all-to-all-start = ((bf16[16,16,768]{2,1,0:T(8,128)(2,1)}), bf16[16,16,768]{2,1,0:T(8,128)(2,1)S(1)}, u32[]{:S(2)}, u32[]{:S(2)}) async-start(bf16[16,16,768]{2,1,0:T(8,128)(2,1)} %bitcast.53), calls=%async_computation | async-start | bytes 786432 | tf_op jit(solution)/shard_map/cond/branch_1_fun/all_to_all | solution.py:106
  24.8 3.2 %collective-permute-start = (bf16[16,4,512]{2,0,1:T(8,128)(2,1)S(1)}, bf16[16,4,512]{2,0,1:T(8,128)(2,1)S(1)}, u32[]{:S(2)}, u32[]{:S(2)}) collective-permute-start(bf16[16,4,512]{2,0,1:T(8,128)(2,1)S(1)} %bitcast.55), channel_id=1, source_target_pairs={{0,1},{1,0},{2,3},{3,2},{4,5},{5,4},{6,7},{7,6},{8,9},{9,8},{10,11... | collective-permute-start | bytes 196616 | tf_op jit(solution)/shard_map/cond/branch_1_fun/ppermute | solution.py:27
  28.0 28.0 %copy-start.1 = (bf16[256,768]{1,0:T(8,128)(2,1)}, bf16[256,768]{1,0:T(8,128)(2,1)S(1)}, u32[]{:S(2)}) copy-start(bf16[256,768]{1,0:T(8,128)(2,1)S(1)} %collective-permute-done.2.next_) | copy-start | bytes 1179652
  28.0 3.2 %collective-permute-start.3 = (bf16[16,4,512]{2,0,1:T(8,128)(2,1)S(1)}, bf16[16,4,512]{2,0,1:T(8,128)(2,1)S(1)}, u32[]{:S(2)}, u32[]{:S(2)}) collective-permute-start(bf16[16,4,512]{2,0,1:T(8,128)(2,1)S(1)} %get-tuple-element.55), channel_id=1, source_target_pairs={{0,2},{2,0},{1,3},{3,1},{4,6},{6,4},{5,7},{7,5},{8,10},{10,8},{9,1... | collective-permute-start | bytes 196616 | tf_op jit(solution)/shard_map/ppermute | solution.py:27
  31.3 9.3 %collective-permute-start.6 = (bf16[16,512]{1,0:T(8,128)(2,1)S(1)}, bf16[16,512]{1,0:T(8,128)(2,1)S(1)}, u32[]{:S(2)}, u32[]{:S(2)}) collective-permute-start(bf16[16,512]{1,0:T(8,128)(2,1)S(1)} %get-tuple-element.52), channel_id=1, source_target_pairs={{0,64},{64,128},{128,192},{192,0},{1,65},{65,129},{129,193},{193,1... | collective-permute-start | bytes 49160 | tf_op jit(solution)/shard_map/ppermute | solution.py:23
  32.8 7.9 %collective-permute-start.5 = (bf16[16,512]{1,0:T(8,128)(2,1)S(1)}, bf16[16,512]{1,0:T(8,128)(2,1)S(1)}, u32[]{:S(2)}, u32[]{:S(2)}) collective-permute-start(bf16[16,512]{1,0:T(8,128)(2,1)S(1)} %get-tuple-element.53), channel_id=1, source_target_pairs={{0,128},{64,192},{128,0},{192,64},{1,129},{65,193},{129,1},{193,65... | collective-permute-start | bytes 49160 | tf_op jit(solution)/shard_map/ppermute | solution.py:23
  35.8 4.8 %collective-permute-start.4 = (bf16[16,512]{1,0:T(8,128)(2,1)S(1)}, bf16[16,512]{1,0:T(8,128)(2,1)S(1)}, u32[]{:S(2)}, u32[]{:S(2)}) collective-permute-start(bf16[16,512]{1,0:T(8,128)(2,1)S(1)} %get-tuple-element.54), channel_id=1, source_target_pairs={{0,192},{64,0},{128,64},{192,128},{1,193},{65,1},{129,65},{193,129... | collective-permute-start | bytes 49160 | tf_op jit(solution)/shard_map/ppermute | solution.py:23
  41.7 22.3 %all-to-all-start.1 = ((bf16[16,64,512]{2,1,0:T(8,128)(2,1)}), bf16[16,64,512]{2,1,0:T(8,128)(2,1)}, u32[]{:S(2)}, u32[]{:S(2)}) async-start(bf16[16,64,512]{2,1,0:T(8,128)(2,1)} %broadcast_in_dim.13), calls=%async_computation.1 | async-start | bytes 2097152 | tf_op jit(solution)/shard_map/all_to_all | solution.py:134
  47.2 8.8 %collective-permute-start.8 = (bf16[128,768]{1,0:T(8,128)(2,1)S(1)}, bf16[128,768]{1,0:T(8,128)(2,1)S(1)}, u32[]{:S(2)}, u32[]{:S(2)}) collective-permute-start(bf16[128,768]{1,0:T(8,128)(2,1)S(1)} %slice.59), channel_id=1, source_target_pairs={{0,64},{64,128},{128,192},{192,0},{1,65},{65,129},{129,193},{193,1... | collective-permute-start | bytes 589832 | tf_op jit(solution)/shard_map/ppermute | solution.py:23
  48.1 8.6 %collective-permute-start.7 = (bf16[128,768]{1,0:T(8,128)(2,1)S(1)}, bf16[128,768]{1,0:T(8,128)(2,1)S(1)}, u32[]{:S(2)}, u32[]{:S(2)}) collective-permute-start(bf16[128,768]{1,0:T(8,128)(2,1)S(1)} %slice.58), channel_id=1, source_target_pairs={{0,192},{64,0},{128,64},{192,128},{1,193},{65,1},{129,65},{193,129... | collective-permute-start | bytes 589832 | tf_op jit(solution)/shard_map/ppermute | solution.py:23
  56.1 0.7 copy-start.3
  56.8 0.7 copy-start.5
  57.4 1.0 %copy-start = (f32[4,256,1]{2,1,0:T(8,128)S(1)}, f32[4,256,1]{2,1,0:T(8,128)}, u32[]{:S(2)}) copy-start(f32[4,256,1]{2,1,0:T(8,128)} %copy.21.valid) | copy-start | bytes 12292
  58.5 1.0 %copy-start.2 = (bf16[256,768]{1,0:T(8,128)(2,1)S(1)}, bf16[256,768]{1,0:T(8,128)(2,1)}, u32[]{:S(2)}) copy-start(bf16[256,768]{1,0:T(8,128)(2,1)} %copy-done.1) | copy-start | bytes 1179652
  59.5 0.9 %copy-start.4 = (bf16[128,768]{1,0:T(8,128)(2,1)S(1)}, bf16[128,768]{1,0:T(8,128)(2,1)}, u32[]{:S(2)}) copy-start(bf16[128,768]{1,0:T(8,128)(2,1)} %copy-done.3) | copy-start | bytes 589828
  60.4 0.9 %copy-start.6 = (bf16[128,768]{1,0:T(8,128)(2,1)S(1)}, bf16[128,768]{1,0:T(8,128)(2,1)}, u32[]{:S(2)}) copy-start(bf16[128,768]{1,0:T(8,128)(2,1)} %copy-done.5) | copy-start | bytes 589828
  64.1 8.4 %collective-permute-start.9 = (bf16[1024,512]{1,0:T(8,128)(2,1)}, bf16[1024,512]{1,0:T(8,128)(2,1)S(1)}, u32[]{:S(2)}, u32[]{:S(2)}) collective-permute-start(bf16[1024,512]{1,0:T(8,128)(2,1)} %bitcast.28.slab), channel_id=1, source_target_pairs={{0,1},{1,0},{2,3},{3,2},{4,5},{5,4},{6,7},{7,6},{8,9},{9,8},{10,11... | collective-permute-start | bytes 3145736 | tf_op jit(solution)/shard_map/ppermute | solution.py:27

commit v3 on v2

v3 whole, which is shorter than its diff:
```python
import functools

import jax
import jax.numpy as jnp
from jax import lax
from jax.experimental import pallas as pl
from jax.experimental.pallas import tpu as pltpu
from jax.sharding import Mesh, PartitionSpec as P

S = 4096
LAG = 256
FRAMES = 1024
W = 768
ROWS = 1024
HALF = 512
AXES = ("tm", "y", "x", "zl", "core")
TILE = ("y", "x", "zl", "core")
F32 = jnp.float32
BF16 = jnp.bfloat16


def shift(value, axis, size, step):
    return lax.ppermute(value, axis, [(i, (i + step) % size) for i in range(size)])


def swap(value, axis):
    return lax.ppermute(value, axis, [(0, 1), (1, 0)])


def columns_kernel(own, next_, prev, far_lo, far_hi, valid, c_out, r_out, sums, held, c_held, r_held, sems, out_sems):
    parts = ((own, held.at[0]), (next_, held.at[1]), (prev, held.at[3]), (far_lo, held.at[2, :128]), (far_hi, held.at[2, 128:]))
    copies = [pltpu.make_async_copy(a, b, sems.at[n]) for n, (a, b) in enumerate(parts)]
    for copy in copies:
        copy.start()
    total = jnp.zeros((1, W), F32)
    for n, block in ((0, 0), (1, 1), (2, 3)):
        copies[n].wait()
        total += jnp.sum(held[block].astype(F32), axis=0, keepdims=True)
    copies[3].wait()
    copies[4].wait()
    total += jnp.sum(held[2].astype(F32), axis=0, keepdims=True)
    mean = total * (1.0 / FRAMES)
    outs = []
    c_total = jnp.zeros((1, W), F32)
    for d in range(4):
        value = (held[d].astype(F32) - mean).astype(BF16)
        c_held[d] = value.reshape(16, 16, W)
        c_total += jnp.sum(value.astype(F32), axis=0, keepdims=True)
        outs.append(pltpu.make_async_copy(c_held.at[d], c_out.at[:, d], out_sems.at[d]))
        outs[-1].start()
    weight = valid[...].T
    r_total = jnp.zeros((1, W), F32)
    for d in range(4):
        e, f = (d + 1) % 4, (d + 3) % 4
        after = c_held[e].reshape(LAG, W).astype(F32) * weight[:, d : d + 1]
        before = c_held[f].reshape(LAG, W).astype(F32) * weight[:, f : f + 1]
        value = (after + before).astype(BF16)
        r_held[d] = value.reshape(16, 16, W)
        r_total += jnp.sum(value.astype(F32), axis=0, keepdims=True)
        outs.append(pltpu.make_async_copy(r_held.at[d], r_out.at[:, d], out_sems.at[4 + d]))
        outs[-1].start()
    sums[:1] = c_total
    sums[1:] = r_total
    for copy in outs:
        copy.wait()


def product_kernel(which, scale, slab, c, r, sums, *refs):
    instant, lagged = refs[-2:]
    left = slab[...].T
    mean = jnp.sum(left.astype(F32), axis=1, keepdims=True) * (1.0 / FRAMES)
    value = jnp.dot(left, c[...], preferred_element_type=F32)
    instant[...] = (value - mean * sums[:1]) * (1.0 / FRAMES)
    value = jnp.dot(left, r[...], preferred_element_type=F32)
    lagged[...] = (value - mean * sums[1:]) * scale[0]


def products(which, scale, slab, c, r, sums, before=()):
    tile = 256
    steps = HALF // tile
    return pl.pallas_call(
        product_kernel,
        grid_spec=pltpu.PrefetchScalarGridSpec(
            num_scalar_prefetch=1,
            grid=(steps,),
            in_specs=[
                pl.BlockSpec(memory_space=pltpu.SMEM),
                pl.BlockSpec((FRAMES, tile), lambda i, w: (0, i)),
                pl.BlockSpec((FRAMES, W), lambda i, w: (0, 0)),
                pl.BlockSpec((FRAMES, W), lambda i, w: (0, 0)),
                pl.BlockSpec((2, W), lambda i, w: (0, 0)),
            ]
            + [pl.BlockSpec(memory_space=pl.ANY)] * len(before),
            out_specs=[pl.BlockSpec((tile, W), lambda i, w: (w[0] * steps + i, 0))] * 2,
        ),
        out_shape=[jax.ShapeDtypeStruct((ROWS, W), F32)] * 2,
        input_output_aliases={6: 0, 7: 1} if before else {},
        compiler_params=pltpu.CompilerParams(vmem_limit_bytes=20 * 2**20),
        cost_estimate=pl.CostEstimate(flops=4 * FRAMES * HALF * W, bytes_accessed=6 * 2**20, transcendentals=0),
        name="products",
    )(which, scale, slab, c, r, sums, *before)


def shards(frames, segments, offset):
    tm = lax.axis_index("tm")
    zl, core = lax.axis_index("zl"), lax.axis_index("core")
    start = offset[0]

    prev = shift(frames, "tm", 4, 1)
    next_ = shift(frames, "tm", 4, -1)

    blocks = segments.reshape(4, LAG)
    valid = jnp.concatenate([blocks[:3] == blocks[1:], jnp.zeros((1, LAG), jnp.bool_)]).astype(F32)
    scale = (0.5 / jnp.sum(valid)).reshape(1)
    valid = lax.dynamic_slice(jnp.concatenate([valid, valid, valid]), (tm, 0), (8, LAG))
    def pick(frames):
        spread = lax.all_to_all(frames.reshape(16, 16, W), ("y", "x"), 0, 0, tiled=True)
        first = jnp.minimum(start // (4 * W), 13)
        mine = lax.dynamic_slice(spread, (first, 0, 0), (3, 16, W))
        column = zl * 2 + core
        zero = jnp.zeros((16, W), BF16)
        row = []
        for p in range(3):
            row += [jnp.where(column == n, mine[p], zero) for n in range(4)]
        row = lax.dynamic_slice(jnp.concatenate(row, axis=1), (0, start - first * 4 * W), (16, S))
        row = row.reshape(16, 4, 2, HALF)
        even = core == 0
        keep = jnp.where(even, row[:, :, 0], row[:, :, 1])
        give = jnp.where(even, row[:, :, 1], row[:, :, 0])
        return keep + swap(give, "core")

    keep = lax.cond(start >= 0, pick, lambda frames: jnp.zeros((16, 4, HALF), BF16), frames)
    keep, prev, next_ = lax.optimization_barrier((keep, prev, next_))
    keep = keep + swap(keep, "zl")

    def block(d):
        return lax.dynamic_slice(keep, (0, lax.rem(tm + d, 4), 0), (16, 1, HALF)).reshape(16, HALF)

    got = {d: shift(block(4 - d), "tm", 4, 4 - d) for d in (2, 1, 3)}
    part = jnp.stack([block(0), got[1], got[2], got[3]])
    part, prev, next_, scale, valid = lax.optimization_barrier((part, prev, next_, scale, valid))
    far_hi = shift(prev[128:], "tm", 4, 1)
    far_lo = shift(next_[:128], "tm", 4, -1)
    part = jnp.broadcast_to(part.reshape(1, 64, HALF), (16, 64, HALF))
    own = lax.all_to_all(part, ("y", "x"), 0, 0, tiled=True).reshape(FRAMES, HALF)

    smem = pl.BlockSpec(memory_space=pltpu.SMEM)
    vmem = pl.BlockSpec(memory_space=pltpu.VMEM)
    c, r, sums = pl.pallas_call(
        columns_kernel,
        out_shape=[jax.ShapeDtypeStruct((16, 4, 16, W), BF16)] * 2 + [jax.ShapeDtypeStruct((2, W), F32)],
        in_specs=[pl.BlockSpec(memory_space=pl.ANY)] * 5 + [vmem],
        out_specs=[pl.BlockSpec(memory_space=pl.ANY)] * 2 + [vmem],
        scratch_shapes=[pltpu.VMEM((4, LAG, W), BF16)]
        + [pltpu.VMEM((4, 16, 16, W), BF16)] * 2
        + [pltpu.SemaphoreType.DMA((5,)), pltpu.SemaphoreType.DMA((8,))],
        compiler_params=pltpu.CompilerParams(vmem_limit_bytes=12 * 2**20),
        cost_estimate=pl.CostEstimate(flops=10**7, bytes_accessed=6 * 2**20, transcendentals=0),
        name="columns",
    )(frames, next_, prev, far_lo, far_hi, valid)
    own, c, r, sums = lax.optimization_barrier((own, c, r, sums))
    other = swap(own, "core")
    c, r = c.reshape(FRAMES, W), r.reshape(FRAMES, W)

    outs = products(core.reshape(1), scale, own, c, r, sums)
    outs = products(1 - core.reshape(1), scale, other, c, r, sums, outs)
    return tuple(outs)


def solution(mesh):
    fine = Mesh(mesh.devices.reshape(4, 4, 4, 2, 2), AXES)
    cut = P("tm", TILE)
    return jax.shard_map(shards, mesh=fine, in_specs=(cut, P(), P()), out_specs=(cut, cut), check_vma=False)
```

time: 76.2 us -> 73.5 us (0.965)
  local copies, waits for them, and re-layouts: 7.67 us -> 2.37 us
  waiting for transfers between devices: 12.9 us -> 16 us
  starting transfers between devices: 38.3 us -> 37.4 us
    unnamed x14 -> x4, local copies, waits for them, and re-layouts: 5.28 us -> 1 us
    ppermute x7, waiting for transfers between devices: 4.18 us -> 6.47 us  [shift(): lax.ppermute(value, axis, [(i, (i + step) % size) for i in range(size)])]
    optimization_barrier x1 -> x0, local copies, waits for them, and re-layouts: 1.02 us -> none  [shards(): lax.optimization_barrier((part, prev, next_, scale, valid, place))]
    all_to_all x1, starting transfers between devices: 5.41 us -> 4.59 us  [shards(): lax.all_to_all(part, ('y', 'x'), 0, 0, tiled=True).reshape(FRAMES, HALF)]
    ppermute x3, waiting for transfers between devices: 2.48 us -> 3.28 us  [swap(): return lax.ppermute(value, axis, [(0, 1), (1, 0)])]
  transfers between devices with their start and end apart: 12 -> 12, of which waited for: 4 -> 5; matrix products, arithmetic and copies ran while one was open for 4% -> 3% of each run, Pallas kernels for 9% -> 10%
where the time goes in v3:
time: 73.5 us; the launch traced here: 73.1 us
  starting transfers between devices  37.4 us (51%)
  waiting for transfers between devices  16 us (22%)
  Pallas kernels  10.4 us (14%)
  loops' own time  2.78 us (4%)
  local copies, waits for them, and re-layouts  2.37 us (3%)
  between operations  2.11 us (3%)
  other arithmetic  1.96 us (3%)
    ppermute x7, starting transfers between devices, shift(): lax.ppermute(value, axis, [(i, (i + step) % size) for i in range(size)])  18.7 us
    ppermute x3, starting transfers between devices, swap(): return lax.ppermute(value, axis, [(0, 1), (1, 0)])  7.35 us
    pallas_call x2, Pallas kernels, products(): pl.pallas_call(product_kernel, grid_spec=pltpu.PrefetchScalarGridSpec(num...  7.15 us
    all_to_all x1, starting transfers between devices, pick(): lax.all_to_all(frames.reshape(16, 16, W), ('y', 'x'), 0, 0, tiled=True)  6.77 us
    ppermute x7, waiting for transfers between devices, shift(): lax.ppermute(value, axis, [(i, (i + step) % size) for i in range(size)])  6.47 us
    all_to_all x1, waiting for transfers between devices, pick(): lax.all_to_all(frames.reshape(16, 16, W), ('y', 'x'), 0, 0, tiled=True)  6.24 us
    all_to_all x1, starting transfers between devices, shards(): lax.all_to_all(part, ('y', 'x'), 0, 0, tiled=True).reshape(FRAMES, HALF)  4.59 us
    pallas_call x1, Pallas kernels, shards(): pl.pallas_call(columns_kernel, out_shape=[jax.ShapeDtypeStruct((16, 4, 16...  3.29 us
  transfers between devices with their start and end apart: 12, of which 5 were waited for; matrix products, arithmetic and copies ran while one was open for 3% of the time, Pallas kernels for 10%

profile of v3, /device:TPU:1, one launch (start us, length us, event | category | flops | bytes accessed | tf_op | source)
XLA Modules:
  0.0 73.1 jit_solution(5918453457957545895)
XLA Ops:
  0.6 3.9 %collective-permute-start.1 = (bf16[256,768]{1,0:T(8,128)(2,1)}, bf16[256,768]{1,0:T(8,128)(2,1)S(1)}, u32[]{:S(2)}, u32[]{:S(2)}) collective-permute-start(bf16[256,768]{1,0:T(8,128)(2,1)} %own.1), channel_id=1, source_target_pairs={{0,64},{64,128},{128,192},{192,0},{1,65},{65,129},{129,193},{193,1... | collective-permute-start | bytes 1179656 | tf_op jit(solution)/shard_map/ppermute | solution.py:23
  4.5 3.1 %collective-permute-start.2 = (bf16[256,768]{1,0:T(8,128)(2,1)}, bf16[256,768]{1,0:T(8,128)(2,1)S(1)}, u32[]{:S(2)}, u32[]{:S(2)}) collective-permute-start(bf16[256,768]{1,0:T(8,128)(2,1)} %own.1), channel_id=1, source_target_pairs={{0,192},{64,0},{128,64},{192,128},{1,193},{65,1},{129,65},{193,129... | collective-permute-start | bytes 1179656 | tf_op jit(solution)/shard_map/ppermute | solution.py:23
  8.3 0.8 %slice_compare_fusion = pred[768]{0:T(1024)(128)(4,1)S(1)} fusion(s32[1024]{0:T(1024)} %param.6), kind=kLoop, calls=%fused_computation.27 | loop fusion | flops 768 | bytes 6912 | tf_op jit(solution)/shard_map/eq | solution.py:113
  9.1 19.7 %conditional.1 = (bf16[16,4,512]{2,0,1:T(8,128)(2,1)S(1)}) conditional(s32[]{:T(128)} %convert_element_type.6, () %tuple.16, (s32[]{:T(128)}, s32[]{:T(128)}, bf16[256,768]{1,0:T(8,128)(2,1)}, s32[]{:T(128)}) %tuple.17), branch_computations={%region_0.0_spmd, %region_1.0_spmd} | conditional | flops 245785 | bytes 3146148 | solution.py:132
  9.1 6.8 %all-to-all-start = ((bf16[16,16,768]{2,1,0:T(8,128)(2,1)}), bf16[16,16,768]{2,1,0:T(8,128)(2,1)S(1)}, u32[]{:S(2)}, u32[]{:S(2)}) async-start(bf16[16,16,768]{2,1,0:T(8,128)(2,1)} %bitcast.53), calls=%async_computation | async-start | bytes 786432 | tf_op jit(solution)/shard_map/cond/branch_1_fun/all_to_all | solution.py:117
  18.5 6.2 %all-to-all-done = bf16[16,16,768]{2,1,0:T(8,128)(2,1)S(1)} async-done(((bf16[16,16,768]{2,1,0:T(8,128)(2,1)}), bf16[16,16,768]{2,1,0:T(8,128)(2,1)S(1)}, u32[]{:S(2)}, u32[]{:S(2)}) %all-to-all-start) | async-done | bytes 393248 | tf_op jit(solution)/shard_map/cond/branch_1_fun/all_to_all | solution.py:117
  25.0 0.1 constant_dynamic-slice_fusion
  25.2 0.1 reshape.88
  25.2 0.3 broadcast_select_fusion.1
  25.6 2.2 %collective-permute-start = (bf16[16,4,512]{2,0,1:T(8,128)(2,1)S(1)}, bf16[16,4,512]{2,0,1:T(8,128)(2,1)S(1)}, u32[]{:S(2)}, u32[]{:S(2)}) collective-permute-start(bf16[16,4,512]{2,0,1:T(8,128)(2,1)S(1)} %bitcast.55), channel_id=1, source_target_pairs={{0,1},{1,0},{2,3},{3,2},{4,5},{5,4},{6,7},{7,6},{8,9},{9,8},{10,11... | collective-permute-start | bytes 196616 | tf_op jit(solution)/shard_map/cond/branch_1_fun/ppermute | solution.py:27
  27.9 0.9 %collective-permute-done = bf16[16,4,512]{2,0,1:T(8,128)(2,1)S(1)} collective-permute-done((bf16[16,4,512]{2,0,1:T(8,128)(2,1)S(1)}, bf16[16,4,512]{2,0,1:T(8,128)(2,1)S(1)}, u32[]{:S(2)}, u32[]{:S(2)}) %collective-permute-start) | collective-permute-done | bytes 65568 | tf_op jit(solution)/shard_map/cond/branch_1_fun/ppermute | solution.py:27
  28.8 0.0 collective-permute-done.1.prev
  28.8 0.0 collective-permute-done.2.next_
  28.8 0.0 copy-start
  28.8 0.8 %collective-permute-start.3 = (bf16[16,4,512]{2,0,1:T(8,128)(2,1)S(1)}, bf16[16,4,512]{2,0,1:T(8,128)(2,1)S(1)}, u32[]{:S(2)}, u32[]{:S(2)}) collective-permute-start(bf16[16,4,512]{2,0,1:T(8,128)(2,1)S(1)} %get-tuple-element.57), channel_id=1, source_target_pairs={{0,2},{2,0},{1,3},{3,1},{4,6},{6,4},{5,7},{7,5},{8,10},{10,8},{9,1... | collective-permute-start | bytes 196616 | tf_op jit(solution)/shard_map/ppermute | solution.py:27
  29.7 2.4 %collective-permute-done.3 = bf16[16,4,512]{2,0,1:T(8,128)(2,1)S(1)} collective-permute-done((bf16[16,4,512]{2,0,1:T(8,128)(2,1)S(1)}, bf16[16,4,512]{2,0,1:T(8,128)(2,1)S(1)}, u32[]{:S(2)}, u32[]{:S(2)}) %collective-permute-start.3) | collective-permute-done | bytes 65568 | tf_op jit(solution)/shard_map/ppermute | solution.py:27
  32.1 1.2 %collective-permute-start.6 = (bf16[16,512]{1,0:T(8,128)(2,1)S(1)}, bf16[16,512]{1,0:T(8,128)(2,1)S(1)}, u32[]{:S(2)}, u32[]{:S(2)}) collective-permute-start(bf16[16,512]{1,0:T(8,128)(2,1)S(1)} %get-tuple-element.54), channel_id=1, source_target_pairs={{0,64},{64,128},{128,192},{192,0},{1,65},{65,129},{129,193},{193,1... | collective-permute-start | bytes 49160 | tf_op jit(solution)/shard_map/ppermute | solution.py:23
  33.3 3.4 %collective-permute-start.5 = (bf16[16,512]{1,0:T(8,128)(2,1)S(1)}, bf16[16,512]{1,0:T(8,128)(2,1)S(1)}, u32[]{:S(2)}, u32[]{:S(2)}) collective-permute-start(bf16[16,512]{1,0:T(8,128)(2,1)S(1)} %get-tuple-element.55), channel_id=1, source_target_pairs={{0,128},{64,192},{128,0},{192,64},{1,129},{65,193},{129,1},{193,65... | collective-permute-start | bytes 49160 | tf_op jit(solution)/shard_map/ppermute | solution.py:23
  36.6 3.5 %collective-permute-start.4 = (bf16[16,512]{1,0:T(8,128)(2,1)S(1)}, bf16[16,512]{1,0:T(8,128)(2,1)S(1)}, u32[]{:S(2)}, u32[]{:S(2)}) collective-permute-start(bf16[16,512]{1,0:T(8,128)(2,1)S(1)} %get-tuple-element.56), channel_id=1, source_target_pairs={{0,192},{64,0},{128,64},{192,128},{1,193},{65,1},{129,65},{193,129... | collective-permute-start | bytes 49160 | tf_op jit(solution)/shard_map/ppermute | solution.py:23
  40.1 0.6 fusion.2
  41.4 0.0 collective-permute-done.6
  41.4 0.0 collective-permute-done.5
  41.5 0.0 collective-permute-done.4
  41.5 1.1 %broadcast_in_dim.9 = bf16[16,64,512]{2,1,0:T(8,128)(2,1)} broadcast(bf16[64,512]{1,0:T(8,128)(2,1)S(1)} %bitcast.54), dimensions={1,2} | broadcast | bytes 1114112 | tf_op jit(solution)/shard_map/broadcast_in_dim | solution.py:144
  42.6 4.6 %all-to-all-start.1 = ((bf16[16,64,512]{2,1,0:T(8,128)(2,1)}), bf16[16,64,512]{2,1,0:T(8,128)(2,1)}, u32[]{:S(2)}, u32[]{:S(2)}) async-start(bf16[16,64,512]{2,1,0:T(8,128)(2,1)} %broadcast_in_dim.9), calls=%async_computation.1 | async-start | bytes 2097152 | tf_op jit(solution)/shard_map/all_to_all | solution.py:145
  47.2 1.7 %collective-permute-start.8 = (bf16[128,768]{1,0:T(8,128)(2,1)S(1)}, bf16[128,768]{1,0:T(8,128)(2,1)S(1)}, u32[]{:S(2)}, u32[]{:S(2)}) collective-permute-start(bf16[128,768]{1,0:T(8,128)(2,1)S(1)} %slice.59), channel_id=1, source_target_pairs={{0,64},{64,128},{128,192},{192,0},{1,65},{65,129},{129,193},{193,1... | collective-permute-start | bytes 589832 | tf_op jit(solution)/shard_map/ppermute | solution.py:23
  48.9 2.0 %collective-permute-start.7 = (bf16[128,768]{1,0:T(8,128)(2,1)S(1)}, bf16[128,768]{1,0:T(8,128)(2,1)S(1)}, u32[]{:S(2)}, u32[]{:S(2)}) collective-permute-start(bf16[128,768]{1,0:T(8,128)(2,1)S(1)} %slice.58), channel_id=1, source_target_pairs={{0,192},{64,0},{128,64},{192,128},{1,193},{65,1},{129,65},{193,129... | collective-permute-start | bytes 589832 | tf_op jit(solution)/shard_map/ppermute | solution.py:23
  50.9 4.6 %collective-permute-done.8.far_hi = bf16[128,768]{1,0:T(8,128)(2,1)S(1)} collective-permute-done((bf16[128,768]{1,0:T(8,128)(2,1)S(1)}, bf16[128,768]{1,0:T(8,128)(2,1)S(1)}, u32[]{:S(2)}, u32[]{:S(2)}) %collective-permute-start.8) | collective-permute-done | bytes 196640 | tf_op jit(solution)/shard_map/ppermute | solution.py:23
  55.4 0.0 copy-done
  55.4 1.9 %collective-permute-done.7.far_lo = bf16[128,768]{1,0:T(8,128)(2,1)S(1)} collective-permute-done((bf16[128,768]{1,0:T(8,128)(2,1)S(1)}, bf16[128,768]{1,0:T(8,128)(2,1)S(1)}, u32[]{:S(2)}, u32[]{:S(2)}) %collective-permute-start.7) | collective-permute-done | bytes 196640 | tf_op jit(solution)/shard_map/ppermute | solution.py:23
  57.3 0.0 copy-start.1
  57.3 1.0 %copy-done.1 = bf16[256,768]{1,0:T(8,128)(2,1)S(1)} copy-done((bf16[256,768]{1,0:T(8,128)(2,1)S(1)}, bf16[256,768]{1,0:T(8,128)(2,1)}, u32[]{:S(2)}) %copy-start.1) | copy-done | bytes 393240
  58.3 3.3 %columns.1 = (bf16[16,4,16,768]{3,2,1,0:T(8,128)(2,1)S(1)}, bf16[16,4,16,768]{3,2,1,0:T(8,128)(2,1)S(1)}, f32[2,768]{1,0:T(2,128)S(1)}) custom-call(bf16[256,768]{1,0:T(8,128)(2,1)} %own.1, bf16[256,768]{1,0:T(8,128)(2,1)S(1)} %copy-done.1, bf16[256,768]{1,0:T(8,128)(2,1)S(1)} %collective-permute-done.1.prev, ...), custom_call_target="tpu_custom_call" | custom-call | flops 10000000 | bytes 6291456 | tf_op jit(solution)/shard_map/columns/pallas_call | solution.py:149
  61.6 0.0 all-to-all-done.1
  61.6 4.3 %collective-permute-start.9 = (bf16[1024,512]{1,0:T(8,128)(2,1)}, bf16[1024,512]{1,0:T(8,128)(2,1)S(1)}, u32[]{:S(2)}, u32[]{:S(2)}) collective-permute-start(bf16[1024,512]{1,0:T(8,128)(2,1)} %bitcast.26.slab), channel_id=1, source_target_pairs={{0,1},{1,0},{2,3},{3,2},{4,5},{5,4},{6,7},{7,6},{8,9},{9,8},{10,11... | collective-permute-start | bytes 3145736 | tf_op jit(solution)/shard_map/ppermute | solution.py:27
  65.9 4.0 %products.2 = (f32[1024,768]{1,0:T(8,128)}, f32[1024,768]{1,0:T(8,128)}) custom-call(s32[1]{0:T(128)} %bitcast.15.which, f32[1]{0:T(128)} %bitcast.24.scale, bf16[1024,512]{1,0:T(8,128)(2,1)} %bitcast.26.slab, bf16[1024,768]{1,0:T(8,128)(2,1)S(1)} %bitcast.49, bf16[1024,768]{1,0:T(8,128)(2,1)S(1)} %bitcast.51, f32[2,768]{1,0:T(2,128)S(1)} %get-tuple-element.48.sums), custom_call_target="tpu_custom_call" | custom-call | flops 1610612736 | bytes 6291456 | tf_op jit(solution)/shard_map/products/pallas_call | solution.py:81
  69.9 0.0 collective-permute-done.9.slab
  70.0 3.1 %products.3 = (f32[1024,768]{1,0:T(8,128)}, f32[1024,768]{1,0:T(8,128)}) custom-call(s32[1]{0:T(128)S(6)} %sub.10.which, f32[1]{0:T(128)} %bitcast.24.scale, bf16[1024,512]{1,0:T(8,128)(2,1)S(1)} %collective-permute-done.9.slab, bf16[1024,768]{1,0:T(8,128)(2,1)S(1)} %bitcast.50, ...), custom_call_target="tpu_custom_call", output_to_operand_aliasing={{0}: (6, {}), {1}: (7, {})} | custom-call | flops 1610612736 | bytes 6291456 | tf_op jit(solution)/shard_map/products/pallas_call | solution.py:81
  (22 shorter events, 0.4 us)
Async XLA Ops:
  0.6 28.2 %collective-permute-start.1 = (bf16[256,768]{1,0:T(8,128)(2,1)}, bf16[256,768]{1,0:T(8,128)(2,1)S(1)}, u32[]{:S(2)}, u32[]{:S(2)}) collective-permute-start(bf16[256,768]{1,0:T(8,128)(2,1)} %own.1), channel_id=1, source_target_pairs={{0,64},{64,128},{128,192},{192,0},{1,65},{65,129},{129,193},{193,1... | collective-permute-start | bytes 1179656 | tf_op jit(solution)/shard_map/ppermute | solution.py:23
  4.5 24.3 %collective-permute-start.2 = (bf16[256,768]{1,0:T(8,128)(2,1)}, bf16[256,768]{1,0:T(8,128)(2,1)S(1)}, u32[]{:S(2)}, u32[]{:S(2)}) collective-permute-start(bf16[256,768]{1,0:T(8,128)(2,1)} %own.1), channel_id=1, source_target_pairs={{0,192},{64,0},{128,64},{192,128},{1,193},{65,1},{129,65},{193,129... | collective-permute-start | bytes 1179656 | tf_op jit(solution)/shard_map/ppermute | solution.py:23
  9.1 15.7 %all-to-all-start = ((bf16[16,16,768]{2,1,0:T(8,128)(2,1)}), bf16[16,16,768]{2,1,0:T(8,128)(2,1)S(1)}, u32[]{:S(2)}, u32[]{:S(2)}) async-start(bf16[16,16,768]{2,1,0:T(8,128)(2,1)} %bitcast.53), calls=%async_computation | async-start | bytes 786432 | tf_op jit(solution)/shard_map/cond/branch_1_fun/all_to_all | solution.py:117
  25.6 3.2 %collective-permute-start = (bf16[16,4,512]{2,0,1:T(8,128)(2,1)S(1)}, bf16[16,4,512]{2,0,1:T(8,128)(2,1)S(1)}, u32[]{:S(2)}, u32[]{:S(2)}) collective-permute-start(bf16[16,4,512]{2,0,1:T(8,128)(2,1)S(1)} %bitcast.55), channel_id=1, source_target_pairs={{0,1},{1,0},{2,3},{3,2},{4,5},{5,4},{6,7},{7,6},{8,9},{9,8},{10,11... | collective-permute-start | bytes 196616 | tf_op jit(solution)/shard_map/cond/branch_1_fun/ppermute | solution.py:27
  28.8 26.6 %copy-start = (bf16[256,768]{1,0:T(8,128)(2,1)}, bf16[256,768]{1,0:T(8,128)(2,1)S(1)}, u32[]{:S(2)}) copy-start(bf16[256,768]{1,0:T(8,128)(2,1)S(1)} %collective-permute-done.2.next_) | copy-start | bytes 1179652
  28.8 3.2 %collective-permute-start.3 = (bf16[16,4,512]{2,0,1:T(8,128)(2,1)S(1)}, bf16[16,4,512]{2,0,1:T(8,128)(2,1)S(1)}, u32[]{:S(2)}, u32[]{:S(2)}) collective-permute-start(bf16[16,4,512]{2,0,1:T(8,128)(2,1)S(1)} %get-tuple-element.57), channel_id=1, source_target_pairs={{0,2},{2,0},{1,3},{3,1},{4,6},{6,4},{5,7},{7,5},{8,10},{10,8},{9,1... | collective-permute-start | bytes 196616 | tf_op jit(solution)/shard_map/ppermute | solution.py:27
  32.1 9.3 %collective-permute-start.6 = (bf16[16,512]{1,0:T(8,128)(2,1)S(1)}, bf16[16,512]{1,0:T(8,128)(2,1)S(1)}, u32[]{:S(2)}, u32[]{:S(2)}) collective-permute-start(bf16[16,512]{1,0:T(8,128)(2,1)S(1)} %get-tuple-element.54), channel_id=1, source_target_pairs={{0,64},{64,128},{128,192},{192,0},{1,65},{65,129},{129,193},{193,1... | collective-permute-start | bytes 49160 | tf_op jit(solution)/shard_map/ppermute | solution.py:23
  33.3 8.2 %collective-permute-start.5 = (bf16[16,512]{1,0:T(8,128)(2,1)S(1)}, bf16[16,512]{1,0:T(8,128)(2,1)S(1)}, u32[]{:S(2)}, u32[]{:S(2)}) collective-permute-start(bf16[16,512]{1,0:T(8,128)(2,1)S(1)} %get-tuple-element.55), channel_id=1, source_target_pairs={{0,128},{64,192},{128,0},{192,64},{1,129},{65,193},{129,1},{193,65... | collective-permute-start | bytes 49160 | tf_op jit(solution)/shard_map/ppermute | solution.py:23
  36.6 4.8 %collective-permute-start.4 = (bf16[16,512]{1,0:T(8,128)(2,1)S(1)}, bf16[16,512]{1,0:T(8,128)(2,1)S(1)}, u32[]{:S(2)}, u32[]{:S(2)}) collective-permute-start(bf16[16,512]{1,0:T(8,128)(2,1)S(1)} %get-tuple-element.56), channel_id=1, source_target_pairs={{0,192},{64,0},{128,64},{192,128},{1,193},{65,1},{129,65},{193,129... | collective-permute-start | bytes 49160 | tf_op jit(solution)/shard_map/ppermute | solution.py:23
  42.6 19.1 %all-to-all-start.1 = ((bf16[16,64,512]{2,1,0:T(8,128)(2,1)}), bf16[16,64,512]{2,1,0:T(8,128)(2,1)}, u32[]{:S(2)}, u32[]{:S(2)}) async-start(bf16[16,64,512]{2,1,0:T(8,128)(2,1)} %broadcast_in_dim.9), calls=%async_computation.1 | async-start | bytes 2097152 | tf_op jit(solution)/shard_map/all_to_all | solution.py:145
  47.2 8.2 %collective-permute-start.8 = (bf16[128,768]{1,0:T(8,128)(2,1)S(1)}, bf16[128,768]{1,0:T(8,128)(2,1)S(1)}, u32[]{:S(2)}, u32[]{:S(2)}) collective-permute-start(bf16[128,768]{1,0:T(8,128)(2,1)S(1)} %slice.59), channel_id=1, source_target_pairs={{0,64},{64,128},{128,192},{192,0},{1,65},{65,129},{129,193},{193,1... | collective-permute-start | bytes 589832 | tf_op jit(solution)/shard_map/ppermute | solution.py:23
  48.9 8.4 %collective-permute-start.7 = (bf16[128,768]{1,0:T(8,128)(2,1)S(1)}, bf16[128,768]{1,0:T(8,128)(2,1)S(1)}, u32[]{:S(2)}, u32[]{:S(2)}) collective-permute-start(bf16[128,768]{1,0:T(8,128)(2,1)S(1)} %slice.58), channel_id=1, source_target_pairs={{0,192},{64,0},{128,64},{192,128},{1,193},{65,1},{129,65},{193,129... | collective-permute-start | bytes 589832 | tf_op jit(solution)/shard_map/ppermute | solution.py:23
  57.3 1.0 %copy-start.1 = (bf16[256,768]{1,0:T(8,128)(2,1)S(1)}, bf16[256,768]{1,0:T(8,128)(2,1)}, u32[]{:S(2)}) copy-start(bf16[256,768]{1,0:T(8,128)(2,1)} %copy-done) | copy-start | bytes 1179652
  61.6 8.3 %collective-permute-start.9 = (bf16[1024,512]{1,0:T(8,128)(2,1)}, bf16[1024,512]{1,0:T(8,128)(2,1)S(1)}, u32[]{:S(2)}, u32[]{:S(2)}) collective-permute-start(bf16[1024,512]{1,0:T(8,128)(2,1)} %bitcast.26.slab), channel_id=1, source_target_pairs={{0,1},{1,0},{2,3},{3,2},{4,5},{5,4},{6,7},{7,6},{8,9},{9,8},{10,11... | collective-permute-start | bytes 3145736 | tf_op jit(solution)/shard_map/ppermute | solution.py:27

commit v4 on v3

--- a/solution.py
+++ b/solution.py
@@ -44,7 +44,8 @@
     c_total = jnp.zeros((1, W), F32)
     for d in range(4):
         value = (held[d].astype(F32) - mean).astype(BF16)
-        c_held[d] = value.reshape(16, 16, W)
+        for g in range(16):
+            c_held[d, g % 4 * 4 + g // 4] = value[16 * g : 16 * g + 16]
         c_total += jnp.sum(value.astype(F32), axis=0, keepdims=True)
         outs.append(pltpu.make_async_copy(c_held.at[d], c_out.at[:, d], out_sems.at[d]))
         outs[-1].start()
@@ -113,6 +114,7 @@
     valid = jnp.concatenate([blocks[:3] == blocks[1:], jnp.zeros((1, LAG), jnp.bool_)]).astype(F32)
     scale = (0.5 / jnp.sum(valid)).reshape(1)
     valid = lax.dynamic_slice(jnp.concatenate([valid, valid, valid]), (tm, 0), (8, LAG))
+    valid = valid.reshape(8, 4, 4, 16).transpose(0, 2, 1, 3).reshape(8, LAG)
     def pick(frames):
         spread = lax.all_to_all(frames.reshape(16, 16, W), ("y", "x"), 0, 0, tiled=True)
         first = jnp.minimum(start // (4 * W), 13)
@@ -142,7 +144,7 @@
     far_hi = shift(prev[128:], "tm", 4, 1)
     far_lo = shift(next_[:128], "tm", 4, -1)
     part = jnp.broadcast_to(part.reshape(1, 64, HALF), (16, 64, HALF))
-    own = lax.all_to_all(part, ("y", "x"), 0, 0, tiled=True).reshape(FRAMES, HALF)
+    own = lax.all_to_all(part, ("x", "y"), 0, 0, tiled=True).reshape(FRAMES, HALF)
 
     smem = pl.BlockSpec(memory_space=pltpu.SMEM)
     vmem = pl.BlockSpec(memory_space=pltpu.VMEM)

time: 73.5 us -> 73.1 us (level)
  no operation moved by 1% of the time
where the time goes in v4:
time: 73.1 us; the launch traced here: 72.6 us
  starting transfers between devices  36.7 us (50%)
  waiting for transfers between devices  16 us (22%)
  Pallas kernels  10.4 us (14%)
  loops' own time  2.78 us (4%)
  local copies, waits for them, and re-layouts  2.59 us (4%)
  between operations  2.12 us (3%)
  other arithmetic  1.97 us (3%)
    ppermute x7, starting transfers between devices, shift(): lax.ppermute(value, axis, [(i, (i + step) % size) for i in range(size)])  18.7 us
    pallas_call x2, Pallas kernels, products(): pl.pallas_call(product_kernel, grid_spec=pltpu.PrefetchScalarGridSpec(num...  7.16 us
    ppermute x3, starting transfers between devices, swap(): return lax.ppermute(value, axis, [(0, 1), (1, 0)])  6.88 us
    all_to_all x1, starting transfers between devices, pick(): lax.all_to_all(frames.reshape(16, 16, W), ('y', 'x'), 0, 0, tiled=True)  6.77 us
    ppermute x7, waiting for transfers between devices, shift(): lax.ppermute(value, axis, [(i, (i + step) % size) for i in range(size)])  6.46 us
    all_to_all x1, waiting for transfers between devices, pick(): lax.all_to_all(frames.reshape(16, 16, W), ('y', 'x'), 0, 0, tiled=True)  6.24 us
    all_to_all x1, starting transfers between devices, shards(): lax.all_to_all(part, ('x', 'y'), 0, 0, tiled=True).reshape(FRAMES, HALF)  4.36 us
    pallas_call x1, Pallas kernels, shards(): pl.pallas_call(columns_kernel, out_shape=[jax.ShapeDtypeStruct((16, 4, 16...  3.29 us
  transfers between devices with their start and end apart: 12, of which 5 were waited for; matrix products, arithmetic and copies ran while one was open for 3% of the time, Pallas kernels for 10%

profile of v4, /device:TPU:1, one launch (start us, length us, event | category | flops | bytes accessed | tf_op | source)
XLA Modules:
  0.0 72.6 jit_solution(2863937977904515605)
XLA Ops:
  0.6 3.9 %collective-permute-start.1 = (bf16[256,768]{1,0:T(8,128)(2,1)}, bf16[256,768]{1,0:T(8,128)(2,1)S(1)}, u32[]{:S(2)}, u32[]{:S(2)}) collective-permute-start(bf16[256,768]{1,0:T(8,128)(2,1)} %own.1), channel_id=1, source_target_pairs={{0,64},{64,128},{128,192},{192,0},{1,65},{65,129},{129,193},{193,1... | collective-permute-start | bytes 1179656 | tf_op jit(solution)/shard_map/ppermute | solution.py:23
  4.5 3.1 %collective-permute-start.2 = (bf16[256,768]{1,0:T(8,128)(2,1)}, bf16[256,768]{1,0:T(8,128)(2,1)S(1)}, u32[]{:S(2)}, u32[]{:S(2)}) collective-permute-start(bf16[256,768]{1,0:T(8,128)(2,1)} %own.1), channel_id=1, source_target_pairs={{0,192},{64,0},{128,64},{192,128},{1,193},{65,1},{129,65},{193,129... | collective-permute-start | bytes 1179656 | tf_op jit(solution)/shard_map/ppermute | solution.py:23
  8.3 0.8 %slice_compare_fusion = pred[768]{0:T(1024)(128)(4,1)S(1)} fusion(s32[1024]{0:T(1024)} %param.6), kind=kLoop, calls=%fused_computation.27 | loop fusion | flops 768 | bytes 6912 | tf_op jit(solution)/shard_map/eq | solution.py:114
  9.1 19.7 %conditional.1 = (bf16[16,4,512]{2,0,1:T(8,128)(2,1)S(1)}) conditional(s32[]{:T(128)} %convert_element_type.6, () %tuple.16, (s32[]{:T(128)}, s32[]{:T(128)}, bf16[256,768]{1,0:T(8,128)(2,1)}, s32[]{:T(128)}) %tuple.17), branch_computations={%region_0.0_spmd, %region_1.0_spmd} | conditional | flops 245785 | bytes 3146148 | solution.py:134
  9.1 6.8 %all-to-all-start = ((bf16[16,16,768]{2,1,0:T(8,128)(2,1)}), bf16[16,16,768]{2,1,0:T(8,128)(2,1)S(1)}, u32[]{:S(2)}, u32[]{:S(2)}) async-start(bf16[16,16,768]{2,1,0:T(8,128)(2,1)} %bitcast.54), calls=%async_computation | async-start | bytes 786432 | tf_op jit(solution)/shard_map/cond/branch_1_fun/all_to_all | solution.py:119
  18.5 6.2 %all-to-all-done = bf16[16,16,768]{2,1,0:T(8,128)(2,1)S(1)} async-done(((bf16[16,16,768]{2,1,0:T(8,128)(2,1)}), bf16[16,16,768]{2,1,0:T(8,128)(2,1)S(1)}, u32[]{:S(2)}, u32[]{:S(2)}) %all-to-all-start) | async-done | bytes 393248 | tf_op jit(solution)/shard_map/cond/branch_1_fun/all_to_all | solution.py:119
  25.0 0.1 constant_dynamic-slice_fusion
  25.2 0.1 reshape.92
  25.2 0.3 broadcast_select_fusion.1
  25.6 2.2 %collective-permute-start = (bf16[16,4,512]{2,0,1:T(8,128)(2,1)S(1)}, bf16[16,4,512]{2,0,1:T(8,128)(2,1)S(1)}, u32[]{:S(2)}, u32[]{:S(2)}) collective-permute-start(bf16[16,4,512]{2,0,1:T(8,128)(2,1)S(1)} %bitcast.57), channel_id=1, source_target_pairs={{0,1},{1,0},{2,3},{3,2},{4,5},{5,4},{6,7},{7,6},{8,9},{9,8},{10,11... | collective-permute-start | bytes 196616 | tf_op jit(solution)/shard_map/cond/branch_1_fun/ppermute | solution.py:27
  27.9 0.9 %collective-permute-done = bf16[16,4,512]{2,0,1:T(8,128)(2,1)S(1)} collective-permute-done((bf16[16,4,512]{2,0,1:T(8,128)(2,1)S(1)}, bf16[16,4,512]{2,0,1:T(8,128)(2,1)S(1)}, u32[]{:S(2)}, u32[]{:S(2)}) %collective-permute-start) | collective-permute-done | bytes 65568 | tf_op jit(solution)/shard_map/cond/branch_1_fun/ppermute | solution.py:27
  28.8 0.0 collective-permute-done.1.prev
  28.8 0.0 collective-permute-done.2.next_
  28.8 0.0 copy-start
  28.8 0.8 %collective-permute-start.3 = (bf16[16,4,512]{2,0,1:T(8,128)(2,1)S(1)}, bf16[16,4,512]{2,0,1:T(8,128)(2,1)S(1)}, u32[]{:S(2)}, u32[]{:S(2)}) collective-permute-start(bf16[16,4,512]{2,0,1:T(8,128)(2,1)S(1)} %get-tuple-element.57), channel_id=1, source_target_pairs={{0,2},{2,0},{1,3},{3,1},{4,6},{6,4},{5,7},{7,5},{8,10},{10,8},{9,1... | collective-permute-start | bytes 196616 | tf_op jit(solution)/shard_map/ppermute | solution.py:27
  29.7 2.4 %collective-permute-done.3 = bf16[16,4,512]{2,0,1:T(8,128)(2,1)S(1)} collective-permute-done((bf16[16,4,512]{2,0,1:T(8,128)(2,1)S(1)}, bf16[16,4,512]{2,0,1:T(8,128)(2,1)S(1)}, u32[]{:S(2)}, u32[]{:S(2)}) %collective-permute-start.3) | collective-permute-done | bytes 65568 | tf_op jit(solution)/shard_map/ppermute | solution.py:27
  32.1 1.2 %collective-permute-start.6 = (bf16[16,512]{1,0:T(8,128)(2,1)S(1)}, bf16[16,512]{1,0:T(8,128)(2,1)S(1)}, u32[]{:S(2)}, u32[]{:S(2)}) collective-permute-start(bf16[16,512]{1,0:T(8,128)(2,1)S(1)} %get-tuple-element.54), channel_id=1, source_target_pairs={{0,64},{64,128},{128,192},{192,0},{1,65},{65,129},{129,193},{193,1... | collective-permute-start | bytes 49160 | tf_op jit(solution)/shard_map/ppermute | solution.py:23
  33.3 3.4 %collective-permute-start.5 = (bf16[16,512]{1,0:T(8,128)(2,1)S(1)}, bf16[16,512]{1,0:T(8,128)(2,1)S(1)}, u32[]{:S(2)}, u32[]{:S(2)}) collective-permute-start(bf16[16,512]{1,0:T(8,128)(2,1)S(1)} %get-tuple-element.55), channel_id=1, source_target_pairs={{0,128},{64,192},{128,0},{192,64},{1,129},{65,193},{129,1},{193,65... | collective-permute-start | bytes 49160 | tf_op jit(solution)/shard_map/ppermute | solution.py:23
  36.6 3.5 %collective-permute-start.4 = (bf16[16,512]{1,0:T(8,128)(2,1)S(1)}, bf16[16,512]{1,0:T(8,128)(2,1)S(1)}, u32[]{:S(2)}, u32[]{:S(2)}) collective-permute-start(bf16[16,512]{1,0:T(8,128)(2,1)S(1)} %get-tuple-element.56), channel_id=1, source_target_pairs={{0,192},{64,0},{128,64},{192,128},{1,193},{65,1},{129,65},{193,129... | collective-permute-start | bytes 49160 | tf_op jit(solution)/shard_map/ppermute | solution.py:23
  40.1 0.1 reshape.108
  40.3 0.1 reshape.109.valid
  40.4 0.6 fusion.2
  41.7 0.0 collective-permute-done.6
  41.7 0.0 collective-permute-done.5
  41.7 0.0 collective-permute-done.4
  41.7 1.1 %broadcast_in_dim.9 = bf16[16,64,512]{2,1,0:T(8,128)(2,1)} broadcast(bf16[64,512]{1,0:T(8,128)(2,1)S(1)} %bitcast.55), dimensions={1,2} | broadcast | bytes 1114112 | tf_op jit(solution)/shard_map/broadcast_in_dim | solution.py:146
  42.8 4.4 %all-to-all-start.1 = ((bf16[16,64,512]{2,1,0:T(8,128)(2,1)}), bf16[16,64,512]{2,1,0:T(8,128)(2,1)}, u32[]{:S(2)}, u32[]{:S(2)}) async-start(bf16[16,64,512]{2,1,0:T(8,128)(2,1)} %broadcast_in_dim.9), calls=%async_computation.1 | async-start | bytes 2097152 | tf_op jit(solution)/shard_map/all_to_all | solution.py:147
  47.2 1.7 %collective-permute-start.8 = (bf16[128,768]{1,0:T(8,128)(2,1)S(1)}, bf16[128,768]{1,0:T(8,128)(2,1)S(1)}, u32[]{:S(2)}, u32[]{:S(2)}) collective-permute-start(bf16[128,768]{1,0:T(8,128)(2,1)S(1)} %slice.59), channel_id=1, source_target_pairs={{0,64},{64,128},{128,192},{192,0},{1,65},{65,129},{129,193},{193,1... | collective-permute-start | bytes 589832 | tf_op jit(solution)/shard_map/ppermute | solution.py:23
  48.9 2.0 %collective-permute-start.7 = (bf16[128,768]{1,0:T(8,128)(2,1)S(1)}, bf16[128,768]{1,0:T(8,128)(2,1)S(1)}, u32[]{:S(2)}, u32[]{:S(2)}) collective-permute-start(bf16[128,768]{1,0:T(8,128)(2,1)S(1)} %slice.58), channel_id=1, source_target_pairs={{0,192},{64,0},{128,64},{192,128},{1,193},{65,1},{129,65},{193,129... | collective-permute-start | bytes 589832 | tf_op jit(solution)/shard_map/ppermute | solution.py:23
  50.9 4.6 %collective-permute-done.8.far_hi = bf16[128,768]{1,0:T(8,128)(2,1)S(1)} collective-permute-done((bf16[128,768]{1,0:T(8,128)(2,1)S(1)}, bf16[128,768]{1,0:T(8,128)(2,1)S(1)}, u32[]{:S(2)}, u32[]{:S(2)}) %collective-permute-start.8) | collective-permute-done | bytes 196640 | tf_op jit(solution)/shard_map/ppermute | solution.py:23
  55.4 0.0 copy-done
  55.4 1.9 %collective-permute-done.7.far_lo = bf16[128,768]{1,0:T(8,128)(2,1)S(1)} collective-permute-done((bf16[128,768]{1,0:T(8,128)(2,1)S(1)}, bf16[128,768]{1,0:T(8,128)(2,1)S(1)}, u32[]{:S(2)}, u32[]{:S(2)}) %collective-permute-start.7) | collective-permute-done | bytes 196640 | tf_op jit(solution)/shard_map/ppermute | solution.py:23
  57.3 0.0 copy-start.1
  57.3 1.0 %copy-done.1 = bf16[256,768]{1,0:T(8,128)(2,1)S(1)} copy-done((bf16[256,768]{1,0:T(8,128)(2,1)S(1)}, bf16[256,768]{1,0:T(8,128)(2,1)}, u32[]{:S(2)}) %copy-start.1) | copy-done | bytes 393240
  58.3 3.3 %columns.1 = (bf16[16,4,16,768]{3,2,1,0:T(8,128)(2,1)S(1)}, bf16[16,4,16,768]{3,2,1,0:T(8,128)(2,1)S(1)}, f32[2,768]{1,0:T(2,128)S(1)}) custom-call(bf16[256,768]{1,0:T(8,128)(2,1)} %own.1, bf16[256,768]{1,0:T(8,128)(2,1)S(1)} %copy-done.1, bf16[256,768]{1,0:T(8,128)(2,1)S(1)} %collective-permute-done.1.prev, ...), custom_call_target="tpu_custom_call" | custom-call | flops 10000000 | bytes 6291456 | tf_op jit(solution)/shard_map/columns/pallas_call | solution.py:151
  61.6 0.0 all-to-all-done.1
  61.6 3.8 %collective-permute-start.9 = (bf16[1024,512]{1,0:T(8,128)(2,1)}, bf16[1024,512]{1,0:T(8,128)(2,1)S(1)}, u32[]{:S(2)}, u32[]{:S(2)}) collective-permute-start(bf16[1024,512]{1,0:T(8,128)(2,1)} %bitcast.27.slab), channel_id=1, source_target_pairs={{0,1},{1,0},{2,3},{3,2},{4,5},{5,4},{6,7},{7,6},{8,9},{9,8},{10,11... | collective-permute-start | bytes 3145736 | tf_op jit(solution)/shard_map/ppermute | solution.py:27
  65.4 4.1 %products.2 = (f32[1024,768]{1,0:T(8,128)}, f32[1024,768]{1,0:T(8,128)}) custom-call(s32[1]{0:T(128)} %bitcast.15.which, f32[1]{0:T(128)} %bitcast.24.scale, bf16[1024,512]{1,0:T(8,128)(2,1)} %bitcast.27.slab, bf16[1024,768]{1,0:T(8,128)(2,1)S(1)} %bitcast.50, bf16[1024,768]{1,0:T(8,128)(2,1)S(1)} %bitcast.52, f32[2,768]{1,0:T(2,128)S(1)} %get-tuple-element.48.sums), custom_call_target="tpu_custom_call" | custom-call | flops 1610612736 | bytes 6291456 | tf_op jit(solution)/shard_map/products/pallas_call | solution.py:82
  69.5 0.0 collective-permute-done.9.slab
  69.5 3.1 %products.3 = (f32[1024,768]{1,0:T(8,128)}, f32[1024,768]{1,0:T(8,128)}) custom-call(s32[1]{0:T(128)S(6)} %sub.10.which, f32[1]{0:T(128)} %bitcast.24.scale, bf16[1024,512]{1,0:T(8,128)(2,1)S(1)} %collective-permute-done.9.slab, bf16[1024,768]{1,0:T(8,128)(2,1)S(1)} %bitcast.51, ...), custom_call_target="tpu_custom_call", output_to_operand_aliasing={{0}: (6, {}), {1}: (7, {})} | custom-call | flops 1610612736 | bytes 6291456 | tf_op jit(solution)/shard_map/products/pallas_call | solution.py:82
  (23 shorter events, 0.4 us)
Async XLA Ops:
  0.6 28.2 %collective-permute-start.1 = (bf16[256,768]{1,0:T(8,128)(2,1)}, bf16[256,768]{1,0:T(8,128)(2,1)S(1)}, u32[]{:S(2)}, u32[]{:S(2)}) collective-permute-start(bf16[256,768]{1,0:T(8,128)(2,1)} %own.1), channel_id=1, source_target_pairs={{0,64},{64,128},{128,192},{192,0},{1,65},{65,129},{129,193},{193,1... | collective-permute-start | bytes 1179656 | tf_op jit(solution)/shard_map/ppermute | solution.py:23
  4.5 24.3 %collective-permute-start.2 = (bf16[256,768]{1,0:T(8,128)(2,1)}, bf16[256,768]{1,0:T(8,128)(2,1)S(1)}, u32[]{:S(2)}, u32[]{:S(2)}) collective-permute-start(bf16[256,768]{1,0:T(8,128)(2,1)} %own.1), channel_id=1, source_target_pairs={{0,192},{64,0},{128,64},{192,128},{1,193},{65,1},{129,65},{193,129... | collective-permute-start | bytes 1179656 | tf_op jit(solution)/shard_map/ppermute | solution.py:23
  9.1 15.7 %all-to-all-start = ((bf16[16,16,768]{2,1,0:T(8,128)(2,1)}), bf16[16,16,768]{2,1,0:T(8,128)(2,1)S(1)}, u32[]{:S(2)}, u32[]{:S(2)}) async-start(bf16[16,16,768]{2,1,0:T(8,128)(2,1)} %bitcast.54), calls=%async_computation | async-start | bytes 786432 | tf_op jit(solution)/shard_map/cond/branch_1_fun/all_to_all | solution.py:119
  25.6 3.2 %collective-permute-start = (bf16[16,4,512]{2,0,1:T(8,128)(2,1)S(1)}, bf16[16,4,512]{2,0,1:T(8,128)(2,1)S(1)}, u32[]{:S(2)}, u32[]{:S(2)}) collective-permute-start(bf16[16,4,512]{2,0,1:T(8,128)(2,1)S(1)} %bitcast.57), channel_id=1, source_target_pairs={{0,1},{1,0},{2,3},{3,2},{4,5},{5,4},{6,7},{7,6},{8,9},{9,8},{10,11... | collective-permute-start | bytes 196616 | tf_op jit(solution)/shard_map/cond/branch_1_fun/ppermute | solution.py:27
  28.8 26.6 %copy-start = (bf16[256,768]{1,0:T(8,128)(2,1)}, bf16[256,768]{1,0:T(8,128)(2,1)S(1)}, u32[]{:S(2)}) copy-start(bf16[256,768]{1,0:T(8,128)(2,1)S(1)} %collective-permute-done.2.next_) | copy-start | bytes 1179652
  28.8 3.2 %collective-permute-start.3 = (bf16[16,4,512]{2,0,1:T(8,128)(2,1)S(1)}, bf16[16,4,512]{2,0,1:T(8,128)(2,1)S(1)}, u32[]{:S(2)}, u32[]{:S(2)}) collective-permute-start(bf16[16,4,512]{2,0,1:T(8,128)(2,1)S(1)} %get-tuple-element.57), channel_id=1, source_target_pairs={{0,2},{2,0},{1,3},{3,1},{4,6},{6,4},{5,7},{7,5},{8,10},{10,8},{9,1... | collective-permute-start | bytes 196616 | tf_op jit(solution)/shard_map/ppermute | solution.py:27
  32.1 9.6 %collective-permute-start.6 = (bf16[16,512]{1,0:T(8,128)(2,1)S(1)}, bf16[16,512]{1,0:T(8,128)(2,1)S(1)}, u32[]{:S(2)}, u32[]{:S(2)}) collective-permute-start(bf16[16,512]{1,0:T(8,128)(2,1)S(1)} %get-tuple-element.54), channel_id=1, source_target_pairs={{0,64},{64,128},{128,192},{192,0},{1,65},{65,129},{129,193},{193,1... | collective-permute-start | bytes 49160 | tf_op jit(solution)/shard_map/ppermute | solution.py:23
  33.3 8.4 %collective-permute-start.5 = (bf16[16,512]{1,0:T(8,128)(2,1)S(1)}, bf16[16,512]{1,0:T(8,128)(2,1)S(1)}, u32[]{:S(2)}, u32[]{:S(2)}) collective-permute-start(bf16[16,512]{1,0:T(8,128)(2,1)S(1)} %get-tuple-element.55), channel_id=1, source_target_pairs={{0,128},{64,192},{128,0},{192,64},{1,129},{65,193},{129,1},{193,65... | collective-permute-start | bytes 49160 | tf_op jit(solution)/shard_map/ppermute | solution.py:23
  36.6 5.1 %collective-permute-start.4 = (bf16[16,512]{1,0:T(8,128)(2,1)S(1)}, bf16[16,512]{1,0:T(8,128)(2,1)S(1)}, u32[]{:S(2)}, u32[]{:S(2)}) collective-permute-start(bf16[16,512]{1,0:T(8,128)(2,1)S(1)} %get-tuple-element.56), channel_id=1, source_target_pairs={{0,192},{64,0},{128,64},{192,128},{1,193},{65,1},{129,65},{193,129... | collective-permute-start | bytes 49160 | tf_op jit(solution)/shard_map/ppermute | solution.py:23
  42.8 18.8 %all-to-all-start.1 = ((bf16[16,64,512]{2,1,0:T(8,128)(2,1)}), bf16[16,64,512]{2,1,0:T(8,128)(2,1)}, u32[]{:S(2)}, u32[]{:S(2)}) async-start(bf16[16,64,512]{2,1,0:T(8,128)(2,1)} %broadcast_in_dim.9), calls=%async_computation.1 | async-start | bytes 2097152 | tf_op jit(solution)/shard_map/all_to_all | solution.py:147
  47.2 8.2 %collective-permute-start.8 = (bf16[128,768]{1,0:T(8,128)(2,1)S(1)}, bf16[128,768]{1,0:T(8,128)(2,1)S(1)}, u32[]{:S(2)}, u32[]{:S(2)}) collective-permute-start(bf16[128,768]{1,0:T(8,128)(2,1)S(1)} %slice.59), channel_id=1, source_target_pairs={{0,64},{64,128},{128,192},{192,0},{1,65},{65,129},{129,193},{193,1... | collective-permute-start | bytes 589832 | tf_op jit(solution)/shard_map/ppermute | solution.py:23
  48.9 8.4 %collective-permute-start.7 = (bf16[128,768]{1,0:T(8,128)(2,1)S(1)}, bf16[128,768]{1,0:T(8,128)(2,1)S(1)}, u32[]{:S(2)}, u32[]{:S(2)}) collective-permute-start(bf16[128,768]{1,0:T(8,128)(2,1)S(1)} %slice.58), channel_id=1, source_target_pairs={{0,192},{64,0},{128,64},{192,128},{1,193},{65,1},{129,65},{193,129... | collective-permute-start | bytes 589832 | tf_op jit(solution)/shard_map/ppermute | solution.py:23
  57.3 1.0 %copy-start.1 = (bf16[256,768]{1,0:T(8,128)(2,1)S(1)}, bf16[256,768]{1,0:T(8,128)(2,1)}, u32[]{:S(2)}) copy-start(bf16[256,768]{1,0:T(8,128)(2,1)} %copy-done) | copy-start | bytes 1179652
  61.6 7.9 %collective-permute-start.9 = (bf16[1024,512]{1,0:T(8,128)(2,1)}, bf16[1024,512]{1,0:T(8,128)(2,1)S(1)}, u32[]{:S(2)}, u32[]{:S(2)}) collective-permute-start(bf16[1024,512]{1,0:T(8,128)(2,1)} %bitcast.27.slab), channel_id=1, source_target_pairs={{0,1},{1,0},{2,3},{3,2},{4,5},{5,4},{6,7},{7,6},{8,9},{9,8},{10,11... | collective-permute-start | bytes 3145736 | tf_op jit(solution)/shard_map/ppermute | solution.py:27
